TPU v7x, 32 devices: a whole 2x2x4 slice. The times are simulated.
32 devices in a mesh: grp: 16 (over z, x, core), tp: 2 (over y).
Axes of the slice: x: 2, y: 2, z: 4, core: 2. Of those that a mesh axis runs over, the one named last changes fastest.
Arguments:
- tokens: bfloat16 [16, 1024, 2048], P(None, 'grp'), may hold values from -6 to 6
- w_query: bfloat16 [2048, 2048], P(None, 'tp'), may hold values from -0.375 to 0.375
- w_key: bfloat16 [2048, 2048], P(None, 'tp'), may hold values from -0.125 to 0.125
- w_value: bfloat16 [2048, 2048], P(None, 'tp'), may hold values from -0.125 to 0.125
- w_out: bfloat16 [2048, 2048], P('tp'), may hold values from -0.125 to 0.125
- own_cache: bfloat16 [16, 2, 2048, 2048], P('grp', None, None, 'tp'), may hold values from -330 to 330
- guest_cache: bfloat16 [16, 2, 2048, 2048], P('grp', None, None, 'tp'), may hold values from -6 to 6
- rec_hidden: bfloat16 [16, 256, 2048], P('grp'), may hold values from -6 to 6
- deal_order: int32 [16], replicated, may hold values from 0 to 15, each once
- own_len: int32 [16], replicated, may hold values from 256 to 2048, as said below
- guest_len: int32 [16], replicated, may hold values from 0 to 2048, as said below
- rec_index: int32 [16, 256], P('grp'), may hold values from 0 to 2047, as said below
Outputs:
- attn_out: bfloat16 [16, 1024, 2048], P(None, 'grp', 'tp')
Inputs may be any that keep to these rules, and one draw needn't show every extreme that they name: Rows 0 to own_len[g] - 1 of group g's own slot hold cached positions 0 to own_len[g] - 1 of the request served at group g; a request whose cache continues in a guest region fills its own slot. The guest_len[g] used rows of group g's guest region continue the cache of the request served at group (g + 8) mod 16. rec_index[g] holds 256 distinct rows of group g's own slot, each below own_len[g].
All inputs are finite; a program needn't handle non-finite values.
Results may differ from a plain program's by a relative error of at most 0.02.
The roundings to bfloat16 on the way count: a program that leaves them out, or rounds other values in their place, can miss the bound.
Values may be sent and summed in bfloat16 or wider, within the bound.
No kernel may reach another device: no remote copies, remote signals or barrier semaphores. Data moves between devices by JAX's collectives and lax.ppermute only.
A program may use at most 192 MiB of HBM per device.

v0:
```python
import jax
import jax.numpy as jnp
from jax import lax
from jax.sharding import PartitionSpec as P

HEAD_DIM = 128


rope_base = 10000.0
norm_eps = 1e-05


def swapped(value, axis, apart):
    mask = 2**apart
    pairs = [(source, source ^ mask) for source in range(lax.axis_size(axis))]
    return lax.ppermute(value, axis, pairs)


def layer_norm(token_rows):
    widened = token_rows.astype(jnp.float32)
    centred = widened - jnp.mean(widened, axis=-1, keepdims=True)
    variance = jnp.mean(centred * centred, axis=-1, keepdims=True)
    return centred * lax.rsqrt(variance + norm_eps)


def rotate(projected, positions, head_dim):
    half_dim = head_dim // 2
    frequency = jnp.exp(-jnp.log(rope_base) * jnp.arange(half_dim, dtype=jnp.float32) / half_dim)
    angles = positions.astype(jnp.float32)[:, None] * frequency[None, :]
    cosine = jnp.cos(angles)[:, None, :]
    sine_part = jnp.sin(angles)[:, None, :]
    shaped = projected.reshape(projected.shape[0], -1, head_dim)
    first_half = shaped[..., :half_dim]
    second = shaped[..., half_dim:]
    turned = jnp.concatenate(
        [first_half * cosine - second * sine_part, second * cosine + first_half * sine_part],
        axis=-1,
    )
    return turned.reshape(projected.shape)


def absorb(softmax_state, queries, key_rows, value_rows, is_valid):
    running_max, weight_sum, numerator = softmax_state
    score_scale = queries.shape[-1] ** (-0.5)
    scores = (
        jnp.einsum("qhd,khd->hqk", queries, key_rows, preferred_element_type=jnp.float32)
        * score_scale
    )
    scores = jnp.where(is_valid[None], scores, -jnp.inf)
    new_max = jnp.maximum(running_max, jnp.max(scores, axis=-1))
    factor = jnp.exp(running_max - new_max)
    expanded = jnp.exp(scores - new_max[..., None])
    weight_sum = weight_sum * factor + jnp.sum(expanded, axis=-1)
    product = jnp.einsum(
        "hqk,khd->qhd",
        expanded.astype(jnp.bfloat16),
        value_rows,
        preferred_element_type=jnp.float32,
    )
    numerator = numerator * jnp.transpose(factor)[:, :, None] + product
    return (new_max, weight_sum, numerator)


def sweep_keys(softmax_state, queries, key_rows, value_rows, live_count):
    block_len = min(512, key_rows.shape[0])
    block_count = (live_count + block_len - 1) // block_len

    def visit_block(block_index, carried):
        block_start = block_index * block_len
        key_block = lax.dynamic_slice_in_dim(key_rows, block_start, block_len, 0)
        value_block = lax.dynamic_slice_in_dim(value_rows, block_start, block_len, 0)
        is_valid = block_start + jnp.arange(block_len, dtype=jnp.int32) < live_count
        return absorb(carried, queries, key_block, value_block, is_valid[None, :])

    return lax.fori_loop(jnp.int32(0), block_count, visit_block, softmax_state)


def shards(
    tokens,
    w_query,
    w_key,
    w_value,
    w_out,
    own_cache,
    guest_cache,
    rec_hidden,
    deal_order,
    own_len,
    guest_len,
    rec_index,
):
    groups = lax.axis_size("grp")
    group_id = lax.axis_index("grp")
    partner_id = (group_id + groups // 2) % groups
    swap_bit = groups.bit_length() - 2
    local_width = w_query.shape[1]
    local_heads = local_width // HEAD_DIM
    arranged = jnp.take(tokens, deal_order, axis=0)
    dealt_rows = lax.all_to_all(arranged, "grp", split_axis=0, concat_axis=1, tiled=True)
    token_rows = dealt_rows[0]
    span_len = token_rows.shape[0]
    own_count = own_len[group_id]
    guest_count = guest_len[partner_id]
    positions = own_count + guest_count + jnp.arange(span_len, dtype=jnp.int32)
    normed = layer_norm(token_rows).astype(jnp.bfloat16)
    queries = rotate(
        jnp.dot(normed, w_query, preferred_element_type=jnp.float32), positions, HEAD_DIM
    ).astype(jnp.bfloat16)
    new_keys = rotate(
        jnp.dot(normed, w_key, preferred_element_type=jnp.float32), positions, HEAD_DIM
    ).astype(jnp.bfloat16)
    new_values = jnp.dot(normed, w_value, preferred_element_type=jnp.float32).astype(jnp.bfloat16)
    rec_rows = layer_norm(rec_hidden[0]).astype(jnp.bfloat16)
    rec_positions = rec_index[0]
    rec_keys = rotate(
        jnp.dot(rec_rows, w_key, preferred_element_type=jnp.float32), rec_positions, HEAD_DIM
    ).astype(jnp.bfloat16)
    rec_values = jnp.dot(rec_rows, w_value, preferred_element_type=jnp.float32).astype(jnp.bfloat16)
    cached_keys = own_cache[0, 0].at[rec_positions].set(rec_keys)
    cached_values = own_cache[0, 1].at[rec_positions].set(rec_values)

    def by_head(matrix):
        return matrix.reshape(matrix.shape[0], local_heads, HEAD_DIM)

    empty_state = (
        jnp.full((local_heads, span_len), -jnp.inf, jnp.float32),
        jnp.zeros((local_heads, span_len), jnp.float32),
        jnp.zeros((span_len, local_heads, HEAD_DIM), jnp.float32),
    )
    causal = jnp.arange(span_len)[None, :] <= jnp.arange(span_len)[:, None]
    query_heads = by_head(queries)
    softmax_state = absorb(empty_state, query_heads, by_head(new_keys), by_head(new_values), causal)
    softmax_state = sweep_keys(
        softmax_state, query_heads, by_head(cached_keys), by_head(cached_values), own_count
    )
    fetched = swapped(guest_cache[0], "grp", swap_bit)
    softmax_state = sweep_keys(
        softmax_state, query_heads, by_head(fetched[0]), by_head(fetched[1]), guest_count
    )
    weight_sum = softmax_state[1]
    numerator = softmax_state[2]
    attended = (
        (numerator / jnp.transpose(weight_sum)[:, :, None])
        .astype(jnp.bfloat16)
        .reshape(span_len, local_width)
    )
    partial_value = jnp.dot(attended, w_out, preferred_element_type=jnp.float32).astype(
        jnp.bfloat16
    )
    summed = lax.psum_scatter(partial_value, "tp", scatter_dimension=1, tiled=True).astype(
        jnp.float32
    )
    mixed_rows = summed.astype(jnp.bfloat16)
    returned_rows = lax.all_to_all(mixed_rows[None], "grp", split_axis=1, concat_axis=0, tiled=True)
    return jnp.zeros_like(returned_rows).at[deal_order].set(returned_rows)


def solution(mesh):
    return jax.shard_map(
        shards,
        mesh=mesh,
        in_specs=(
            P(None, "grp", None),
            P(None, "tp"),
            P(None, "tp"),
            P(None, "tp"),
            P("tp", None),
            P("grp", None, None, "tp"),
            P("grp", None, None, "tp"),
            P("grp", None, None),
            P(),
            P(),
            P(),
            P("grp", None),
        ),
        out_specs=P(None, "grp", "tp"),
        check_vma=False,
    )
```

profile of v0, /device:TPU:0, one launch (start us, length us, event | category | flops | bytes accessed | tf_op | source)
XLA Modules:
  0.0 714.4 jit_solution(7556308025634775510)
XLA Ops:
  17.4 7.4 %all-to-all-start = ((bf16[16,64,2048]{2,1,0:T(8,128)(2,1)}), bf16[16,64,2048]{2,1,0:T(8,128)(2,1)}, u32[]{:S(2)}, u32[]{:S(2)}) async-start(bf16[16,64,2048]{2,1,0:T(8,128)(2,1)} %broadcast_select_fusion), calls=%async_computation | async-start | bytes 8388608 | tf_op jit(solution)/shard_map/all_to_all | solution.py:99
  24.9 11.7 %copy.72 = bf16[1,2,2048,1024]{2,3,1,0:T(8,128)(2,1)} copy(bf16[1,2,2048,1024]{3,2,1,0:T(8,128)(2,1)} %param.22) | data formatting | bytes 16777216 | tf_op args[6]
  43.0 6.5 copy.82
  49.5 6.6 copy.81
  61.1 5.9 slice_bitcast_fusion
  67.1 6.5 scatter_fusion
  73.6 6.5 copy.68
  83.6 6.8 scatter_fusion.1
  90.4 6.5 copy.69
  98.2 184.1 %all-to-all-done = bf16[16,64,2048]{2,1,0:T(8,128)(2,1)} async-done(((bf16[16,64,2048]{2,1,0:T(8,128)(2,1)}), bf16[16,64,2048]{2,1,0:T(8,128)(2,1)}, u32[]{:S(2)}, u32[]{:S(2)}) %all-to-all-start) | async-done | bytes 4194336 | tf_op jit(solution)/shard_map/all_to_all | solution.py:99
  304.3 13.8 %fusion.38 = (f32[8,1024]{1,0:T(8,128)S(1)}, f32[8,1024,1024]{1,2,0:T(8,128)}) fusion(pred[1024,1024]{0,1:T(8,128)(4,1)S(1)} %iota_compare_fusion, bf16[1024,8,64]{0,2,1:T(8,128)(2,1)S(1)} %get-tuple-element.235, bf16[1024,8,64]{0,2,1:T(8,128)(2,1)S(1)} %get-tuple-element.236, bf16[1024,8,64]{0,2,1:T(8,128)(2,1)S(1)} %get-tuple-element.230, ...), kind=kOutput, calls=%fused_computation.52 | convolution fusion | flops 2181029888 | bytes 38830080 | tf_op jit(solution)/shard_map/qhd,khd->hqk/dot_general | solution.py:46
  318.1 26.7 %fusion.40 = f32[8,1024]{1,0:T(8,128)S(1)} fusion(f32[8,1024,1024]{1,2,0:T(8,128)} %get-tuple-element.244, f32[8,1024]{1,0:T(8,128)S(1)} %get-tuple-element.374, pred[1024,1024]{0,1:T(8,128)(4,1)S(1)} %iota_compare_fusion), kind=kLoop, calls=%fused_computation.54 | loop fusion | flops 33546240 | bytes 34668544 | tf_op jit(solution)/shard_map/reduce_sum | solution.py:53
  348.3 5.8 convolution_convert_fusion.1
  357.1 17.1 %bitcast_add_fusion.2 = f32[1024,8,128]{0,2,1:T(8,128)} fusion(bf16[1024,8,128]{0,2,1:T(8,128)(2,1)} %bitcast.150, f32[8,1024,1024]{1,2,0:T(8,128)} %get-tuple-element.244, f32[8,1024]{1,0:T(8,128)S(1)} %get-tuple-element.374, pred[1024,1024]{0,1:T(8,128)(4,1)} %copy-done, f32[1024,8]{0,1:T(8,128)S(1)} %get-tuple-element.237), kind=kOutput, calls=%fused_computation.63 | convolution fusion | flops 2182086656 | bytes 40960000 | tf_op jit(solution)/shard_map/hqk,khd->qhd/dot_general | solution.py:54
  374.2 68.9 %while.28 = (s32[]{:T(128)}, f32[8,1024]{1,0:T(8,128)S(1)}, f32[8,1024]{1,0:T(8,128)S(1)}, f32[1024,8,128]{0,2,1:T(8,128)}, s32[]{:T(128)}, /*index=5*/s32[]{:T(...) while((s32[]{:T(128)}, f32[8,1024]{1,0:T(8,128)S(1)}, ...), condition=%wide.region_11.12_spmd, body=%wide.region_8.11_spmd.sunk | while | flops 2195743744 | bytes 63441084 | solution.py:75
  379.8 7.8 %bitcast_add_fusion.5 = f32[1024,8,128]{0,2,1:T(8,128)} fusion(f32[1024,8,128]{0,2,1:T(8,128)} %get-tuple-element.389, f32[8,512,1024]{2,1,0:T(8,128)S(1)} %get-tuple-element.358, f32[8,1024]{1,0:T(8,128)S(1)} %get-tuple-element.400, pred[512]{0:T(512)(128)(4,1)S(1)} %add_compare_fusion.4, f32[1024,8]{0,1:T(8,128)S(1)} %get-tuple-element.359, ...), kind=kOutput, calls=%fused_computation.15.clone.1 | convolution fusion | flops 1092616192 | bytes 26280452 | tf_op jit(solution)/shard_map/while/body/hqk,khd->qhd/dot_general | solution.py:54
  397.0 7.8 %bitcast_add_fusion.5 = f32[1024,8,128]{0,2,1:T(8,128)} fusion(f32[1024,8,128]{0,2,1:T(8,128)} %get-tuple-element.389, f32[8,512,1024]{2,1,0:T(8,128)S(1)} %get-tuple-element.358, f32[8,1024]{1,0:T(8,128)S(1)} %get-tuple-element.400, pred[512]{0:T(512)(128)(4,1)S(1)} %add_compare_fusion.4, f32[1024,8]{0,1:T(8,128)S(1)} %get-tuple-element.359, ...), kind=kOutput, calls=%fused_computation.15.clone.1 | convolution fusion | flops 1092616192 | bytes 26280452 | tf_op jit(solution)/shard_map/while/body/hqk,khd->qhd/dot_general | solution.py:54
  414.3 7.8 %bitcast_add_fusion.5 = f32[1024,8,128]{0,2,1:T(8,128)} fusion(f32[1024,8,128]{0,2,1:T(8,128)} %get-tuple-element.389, f32[8,512,1024]{2,1,0:T(8,128)S(1)} %get-tuple-element.358, f32[8,1024]{1,0:T(8,128)S(1)} %get-tuple-element.400, pred[512]{0:T(512)(128)(4,1)S(1)} %add_compare_fusion.4, f32[1024,8]{0,1:T(8,128)S(1)} %get-tuple-element.359, ...), kind=kOutput, calls=%fused_computation.15.clone.1 | convolution fusion | flops 1092616192 | bytes 26280452 | tf_op jit(solution)/shard_map/while/body/hqk,khd->qhd/dot_general | solution.py:54
  431.5 7.8 %bitcast_add_fusion.5 = f32[1024,8,128]{0,2,1:T(8,128)} fusion(f32[1024,8,128]{0,2,1:T(8,128)} %get-tuple-element.389, f32[8,512,1024]{2,1,0:T(8,128)S(1)} %get-tuple-element.358, f32[8,1024]{1,0:T(8,128)S(1)} %get-tuple-element.400, pred[512]{0:T(512)(128)(4,1)S(1)} %add_compare_fusion.4, f32[1024,8]{0,1:T(8,128)S(1)} %get-tuple-element.359, ...), kind=kOutput, calls=%fused_computation.15.clone.1 | convolution fusion | flops 1092616192 | bytes 26280452 | tf_op jit(solution)/shard_map/while/body/hqk,khd->qhd/dot_general | solution.py:54
  443.1 35.4 %collective-permute-done = bf16[2,2048,1024]{1,2,0:T(8,128)(2,1)} collective-permute-done((bf16[2,2048,1024]{1,2,0:T(8,128)(2,1)}, bf16[2,2048,1024]{1,2,0:T(8,128)(2,1)}, u32[]{:S(2)}, u32[]{:S(2)}) %collective-permute-start) | collective-permute-done | bytes 8388640 | tf_op jit(solution)/shard_map/ppermute | solution.py:16
  478.5 6.0 fusion.72
  484.5 68.9 %while.29 = (s32[]{:T(128)}, f32[8,1024]{1,0:T(8,128)S(1)}, f32[8,1024]{1,0:T(8,128)S(1)}, f32[1024,8,128]{0,2,1:T(8,128)}, s32[]{:T(128)}, /*index=5*/s32[]{:T(...) while((s32[]{:T(128)}, f32[8,1024]{1,0:T(8,128)S(1)}, ...), condition=%wide.region_15.16_spmd, body=%wide.region_12.15_spmd.sunk | while | flops 2195743744 | bytes 63441084 | solution.py:75
  490.1 7.8 %bitcast_add_fusion.6 = f32[1024,8,128]{0,2,1:T(8,128)} fusion(f32[1024,8,128]{0,2,1:T(8,128)} %get-tuple-element.428, f32[8,512,1024]{2,1,0:T(8,128)S(1)} %get-tuple-element.371, f32[8,1024]{1,0:T(8,128)S(1)} %get-tuple-element.439, pred[512]{0:T(512)(128)(4,1)S(1)} %add_compare_fusion.5, f32[1024,8]{0,1:T(8,128)S(1)} %get-tuple-element.372, ...), kind=kOutput, calls=%fused_computation.38.clone.1 | convolution fusion | flops 1092616192 | bytes 26280452 | tf_op jit(solution)/shard_map/while/body/hqk,khd->qhd/dot_general | solution.py:54
  507.2 7.8 %bitcast_add_fusion.6 = f32[1024,8,128]{0,2,1:T(8,128)} fusion(f32[1024,8,128]{0,2,1:T(8,128)} %get-tuple-element.428, f32[8,512,1024]{2,1,0:T(8,128)S(1)} %get-tuple-element.371, f32[8,1024]{1,0:T(8,128)S(1)} %get-tuple-element.439, pred[512]{0:T(512)(128)(4,1)S(1)} %add_compare_fusion.5, f32[1024,8]{0,1:T(8,128)S(1)} %get-tuple-element.372, ...), kind=kOutput, calls=%fused_computation.38.clone.1 | convolution fusion | flops 1092616192 | bytes 26280452 | tf_op jit(solution)/shard_map/while/body/hqk,khd->qhd/dot_general | solution.py:54
  524.4 7.8 %bitcast_add_fusion.6 = f32[1024,8,128]{0,2,1:T(8,128)} fusion(f32[1024,8,128]{0,2,1:T(8,128)} %get-tuple-element.428, f32[8,512,1024]{2,1,0:T(8,128)S(1)} %get-tuple-element.371, f32[8,1024]{1,0:T(8,128)S(1)} %get-tuple-element.439, pred[512]{0:T(512)(128)(4,1)S(1)} %add_compare_fusion.5, f32[1024,8]{0,1:T(8,128)S(1)} %get-tuple-element.372, ...), kind=kOutput, calls=%fused_computation.38.clone.1 | convolution fusion | flops 1092616192 | bytes 26280452 | tf_op jit(solution)/shard_map/while/body/hqk,khd->qhd/dot_general | solution.py:54
  541.6 7.8 %bitcast_add_fusion.6 = f32[1024,8,128]{0,2,1:T(8,128)} fusion(f32[1024,8,128]{0,2,1:T(8,128)} %get-tuple-element.428, f32[8,512,1024]{2,1,0:T(8,128)S(1)} %get-tuple-element.371, f32[8,1024]{1,0:T(8,128)S(1)} %get-tuple-element.439, pred[512]{0:T(512)(128)(4,1)S(1)} %add_compare_fusion.5, f32[1024,8]{0,1:T(8,128)S(1)} %get-tuple-element.372, ...), kind=kOutput, calls=%fused_computation.38.clone.1 | convolution fusion | flops 1092616192 | bytes 26280452 | tf_op jit(solution)/shard_map/while/body/hqk,khd->qhd/dot_general | solution.py:54
  556.9 6.2 convolution_convert_fusion
  563.1 51.7 %reduce-scatter.2.cloned.1.call-done = bf16[1024,1024]{1,0:T(8,128)(2,1)} async-done(((bf16[1024,2048]{1,0:T(8,128)(2,1)}), bf16[1024,1024]{1,0:T(8,128)(2,1)}) %reduce-scatter.2.cloned.1.call-update) | async-done | bytes 2097168 | tf_op jit(solution)/shard_map/reduce_scatter | solution.py:150
  614.9 6.7 copy.87
  622.1 12.8 %reduce.9 = bf16[1024,1024]{1,0:T(8,128)(2,1)S(1)} reduce(bf16[1024,1,1024]{2,1,0:T(2,128)(2,1)} %bitcast.132, bf16[]{:T(256)} %broadcast.273), dimensions={1}, to_apply=%bitcast.103.reduce_sub_computation | reduce | bytes 4194306
  637.7 52.9 %all_to_all.21 = bf16[16,2,32768]{2,1,0:T(2,128)(2,1)S(1)} all-to-all(bf16[16,2,32768]{2,1,0:T(2,128)(2,1)} %reshape.350), channel_id=1, replica_groups=mesh['grp'=16,'tp'=2] {'grp'}, dimensions={0} | all-to-all | bytes 4194304 | tf_op jit(solution)/shard_map/all_to_all | solution.py:154
  690.6 6.8 reshape.351
  (116 shorter events, 144.2 us)
Async XLA Ops:
  7.2 0.7 copy-start.5
  17.4 264.9 %all-to-all-start = ((bf16[16,64,2048]{2,1,0:T(8,128)(2,1)}), bf16[16,64,2048]{2,1,0:T(8,128)(2,1)}, u32[]{:S(2)}, u32[]{:S(2)}) async-start(bf16[16,64,2048]{2,1,0:T(8,128)(2,1)} %broadcast_select_fusion), calls=%async_computation | async-start | bytes 8388608 | tf_op jit(solution)/shard_map/all_to_all | solution.py:99
  24.9 14.6 %copy-start.9 = (s32[16]{0:T(128)S(1)}, s32[16]{0:T(128)}, u32[]{:S(2)}) copy-start(s32[16]{0:T(128)} %param.25) | copy-start | bytes 196
  24.9 15.8 %copy-start.10 = (s32[16]{0:T(128)S(1)}, s32[16]{0:T(128)}, u32[]{:S(2)}) copy-start(s32[16]{0:T(128)} %param.26) | copy-start | bytes 196
  24.9 590.0 %reduce-scatter.2.cloned.1.call-start = ((), (), s32[]{:S(2)}) async-start(), calls=%async_computation.3 | async-start | bytes 6291456 | tf_op jit(solution)/shard_map/reduce_scatter | solution.py:150
  36.7 441.8 %collective-permute-start = (bf16[2,2048,1024]{1,2,0:T(8,128)(2,1)}, bf16[2,2048,1024]{1,2,0:T(8,128)(2,1)}, u32[]{:S(2)}, u32[]{:S(2)}) collective-permute-start(bf16[2,2048,1024]{1,2,0:T(8,128)(2,1)} %bitcast.135), channel_id=1, source_target_pairs={{0,16},{2,18},{4,20},{6,22},{8,24},{10,26},{12,28},{14,30},{16,0},... | collective-permute-start | bytes 25165832 | tf_op jit(solution)/shard_map/ppermute | solution.py:16
  49.5 6.6 copy-start.4
  49.5 6.6 copy-start.3
  97.2 220.9 %copy-start = (pred[1024,1024]{0,1:T(8,128)(4,1)}, pred[1024,1024]{0,1:T(8,128)(4,1)S(1)}, u32[]{:S(2)}) copy-start(pred[1024,1024]{0,1:T(8,128)(4,1)S(1)} %iota_compare_fusion) | copy-start | bytes 3145732
  288.7 3.5 copy-start.2
  292.2 4.5 copy-start.1
  344.8 3.5 copy-start.7
  553.4 3.5 copy-start.8
  697.4 4.6 copy-start.6
Sparse Core Ops, SparseCore 0:
  563.3 51.5 reduce-scatter.1
where the time goes:
time: 725 us; the launch traced here: 714 us
  waiting for transfers between devices  271 us (37%)
  matrix products  161 us (22%)
  other arithmetic  101 us (14%)
  local copies, waits for them, and re-layouts  101 us (14%)
  blocking collectives  52.9 us (7%)
  between operations  16.4 us (2%)
  starting transfers between devices  10.2 us (1%)
    all_to_all x1, waiting for transfers between devices, shards(): lax.all_to_all(arranged, 'grp', split_axis=0, concat_axis=1, tiled=True)  184 us
    dot_general x9, matrix products, absorb(): jnp.einsum('hqk,khd->qhd', expanded.astype(jnp.bfloat16), value_rows, pre...  79.5 us
    reduce_sum x9, other arithmetic, absorb(): weight_sum = weight_sum * factor + jnp.sum(expanded, axis=-1)  56.9 us
    dot_general x9, matrix products, absorb(): jnp.einsum('qhd,khd->hqk', queries, key_rows, preferred_element_type=jnp....  53.4 us
    all_to_all x1, blocking collectives, shards(): lax.all_to_all(mixed_rows[None], 'grp', split_axis=1, concat_axis=0, tile...  52.9 us
    reduce_scatter x1, waiting for transfers between devices, shards(): lax.psum_scatter(partial_value, 'tp', scatter_dimension=1, tiled=True)  51.7 us
    ppermute x1, waiting for transfers between devices, swapped(): return lax.ppermute(value, axis, pairs)  35.4 us
    unnamed x27, local copies, waits for them, and re-layouts  26.3 us
  transfers between devices with their start and end apart: 3, of which 3 were waited for; matrix products, arithmetic and copies ran while one was open for 32% of the time, Pallas kernels for 0%

commit v1 on v0

v1 whole, which is shorter than its diff:
```python
import functools
import math

import jax
import jax.numpy as jnp
from jax import lax
from jax.experimental import pallas as pl
from jax.experimental.pallas import tpu as pltpu
from jax.sharding import PartitionSpec as P

HEAD_DIM = 128
KEY_BLOCK = 512
ROW_BLOCK = 256
VMEM_LIMIT = 50 * 1024 * 1024

rope_base = 10000.0
norm_eps = 1e-05
LOG2E = math.log2(math.e)
LOWEST = -1e30


def params():
    return pltpu.CompilerParams(vmem_limit_bytes=VMEM_LIMIT)


def layer_norm(token_rows):
    widened = token_rows.astype(jnp.float32)
    centred = widened - jnp.mean(widened, axis=-1, keepdims=True)
    variance = jnp.mean(centred * centred, axis=-1, keepdims=True)
    return centred * lax.rsqrt(variance + norm_eps)


def rope_tables(positions):
    half_dim = HEAD_DIM // 2
    frequency = jnp.exp(-jnp.log(rope_base) * jnp.arange(half_dim, dtype=jnp.float32) / half_dim)
    angles = positions.astype(jnp.float32)[:, None] * frequency[None, :]
    cosine = jnp.cos(angles)
    sine = jnp.sin(angles)
    return (
        jnp.concatenate([cosine, cosine], axis=-1),
        jnp.concatenate([-sine, sine], axis=-1),
    )


def deal_kernel(deal_ref, tp_ref, x_ref, own_ref, guest_ref):
    normed = layer_norm(x_ref[0]).astype(jnp.bfloat16)
    own_ref[0] = normed
    guest_ref[0] = normed


def deal(tokens, deal_order, tp_index, piece):
    groups, _, width = tokens.shape
    half = groups // 2
    out = jax.ShapeDtypeStruct((groups, piece, width), jnp.bfloat16)
    return pl.pallas_call(
        deal_kernel,
        grid_spec=pltpu.PrefetchScalarGridSpec(
            num_scalar_prefetch=2,
            grid=(groups,),
            in_specs=[pl.BlockSpec((1, piece, width), lambda d, order, t: (order[d], t[0], 0))],
            out_specs=[
                pl.BlockSpec((1, piece, width), lambda d, order, t: (d, 0, 0)),
                pl.BlockSpec((1, piece, width), lambda d, order, t: ((d + half) % groups, 0, 0)),
            ],
        ),
        out_shape=[out, out],
        compiler_params=params(),
        name="deal",
    )(deal_order, tp_index, tokens)


def project_kernel(turned, heads, x_ref, cos_ref, sin_ref, *refs):
    count = len(turned)
    x = x_ref[...]
    for w_ref, out_ref, turn in zip(refs[:count], refs[count:], turned):
        product = jnp.dot(x, w_ref[...], preferred_element_type=jnp.float32)
        if not turn:
            out_ref[...] = product.astype(jnp.bfloat16)
            continue
        for head in range(heads):
            cut = slice(head * HEAD_DIM, (head + 1) * HEAD_DIM)
            part = product[:, cut]
            swapped = pltpu.roll(part, HEAD_DIM // 2, 1)
            out_ref[:, cut] = (part * cos_ref[...] + swapped * sin_ref[...]).astype(jnp.bfloat16)


def project(x, tables, weights, turned):
    rows, depth = x.shape
    width = weights[0].shape[1]
    block = min(256, width)
    whole = pl.BlockSpec((rows, depth), lambda n: (0, 0))
    table = pl.BlockSpec((rows, HEAD_DIM), lambda n: (0, 0))
    count = len(weights)
    return pl.pallas_call(
        functools.partial(project_kernel, turned, block // HEAD_DIM),
        grid=(width // block,),
        in_specs=[whole, table, table] + [pl.BlockSpec((depth, block), lambda n: (0, n))] * count,
        out_specs=[pl.BlockSpec((rows, block), lambda n: (0, n))] * count,
        out_shape=[jax.ShapeDtypeStruct((rows, width), jnp.bfloat16)] * count,
        compiler_params=params(),
        cost_estimate=pl.CostEstimate(
            flops=2 * rows * depth * width * count,
            bytes_accessed=2 * (rows * depth + count * width * (rows + depth)),
            transcendentals=0,
        ),
        name="project",
    )(x, *tables, *weights)


def replace_kernel(block, index_ref, cache_ref, fresh_ref, out_ref):
    first = pl.program_id(1) * block
    count = index_ref.shape[1]
    row = first + lax.broadcasted_iota(jnp.int32, (block, count), 0)
    hits = jnp.where(row == index_ref[...], 1.0, 0.0)
    picked = jnp.dot(
        hits.astype(jnp.bfloat16), fresh_ref[0], preferred_element_type=jnp.float32
    )
    is_hit = jnp.sum(hits, axis=1, keepdims=True) > 0.5
    out_ref[0] = jnp.where(is_hit, picked, cache_ref[0, 0].astype(jnp.float32)).astype(jnp.bfloat16)


def replace_rows(cache, fresh, rec_index):
    _, _, rows, width = cache.shape
    count = rec_index.shape[1]
    block = 512
    return pl.pallas_call(
        functools.partial(replace_kernel, block),
        grid=(2, rows // block),
        in_specs=[
            pl.BlockSpec((1, count), lambda c, r: (0, 0)),
            pl.BlockSpec((1, 1, block, width), lambda c, r: (0, c, r, 0)),
            pl.BlockSpec((1, count, width), lambda c, r: (c, 0, 0)),
        ],
        out_specs=pl.BlockSpec((1, block, width), lambda c, r: (c, r, 0)),
        out_shape=jax.ShapeDtypeStruct((2, rows, width), jnp.bfloat16),
        compiler_params=params(),
        name="replace_rows",
    )(rec_index, cache, fresh)


def fold_block(rows, scale, q_ref, m_ref, acc_ref, keys, values, mask):
    ones = jnp.ones(values.shape, jnp.bfloat16)
    widened = jnp.concatenate([values, ones], axis=1)
    q = q_ref[rows, :]
    scores = lax.dot_general(
        q, keys, (((1,), (1,)), ((), ())), preferred_element_type=jnp.float32
    )
    if mask is not None:
        scores = jnp.where(mask, scores, LOWEST)
    old_max = m_ref[rows, :]
    new_max = jnp.maximum(old_max, jnp.max(scores, axis=1, keepdims=True))
    factor = jnp.exp2((old_max - new_max) * scale)
    shift = new_max[:, :1] * scale
    weights = jnp.exp2(scores * scale - shift).astype(jnp.bfloat16)
    product = jnp.dot(weights, widened, preferred_element_type=jnp.float32)
    acc_ref[rows, :] = acc_ref[rows, :] * jnp.concatenate([factor, factor], axis=1) + product
    m_ref[rows, :] = new_max


def attend_kernel(causal, count_ref, q_ref, k_ref, v_ref, *refs):
    if causal:
        nk_ref, nv_ref, o_ref, lse_ref, m_ref, acc_ref = refs
    else:
        o_ref, lse_ref, m_ref, acc_ref = refs
    head = pl.program_id(0)
    scale = HEAD_DIM**-0.5 * LOG2E
    span = q_ref.shape[0]
    used = count_ref[0]
    parts = [pl.ds(i * ROW_BLOCK, ROW_BLOCK) for i in range(span // ROW_BLOCK)]
    m_ref[...] = jnp.full(m_ref.shape, LOWEST, jnp.float32)
    acc_ref[...] = jnp.zeros(acc_ref.shape, jnp.float32)
    cache = k_ref.at[(0,) * (len(k_ref.shape) - 2)], v_ref.at[(0,) * (len(v_ref.shape) - 2)]

    def visit(block, masked):
        start = pl.multiple_of(block * KEY_BLOCK, KEY_BLOCK)
        keys = cache[0][pl.ds(start, KEY_BLOCK), :]
        values = cache[1][pl.ds(start, KEY_BLOCK), :]
        mask = None
        if masked:
            place = lax.broadcasted_iota(jnp.int32, (1, KEY_BLOCK), 1)
            mask = place < used - start
        for rows in parts:
            fold_block(rows, scale, q_ref, m_ref, acc_ref, keys, values, mask)

    full = used // KEY_BLOCK
    pl.loop(0, full)(lambda block: visit(block, False))

    @pl.when(used % KEY_BLOCK > 0)
    def _():
        visit(full, True)

    if causal:
        for i, rows in enumerate(parts):
            width = (i + 1) * ROW_BLOCK
            key_at = lax.broadcasted_iota(jnp.int32, (ROW_BLOCK, width), 1)
            row_at = lax.broadcasted_iota(jnp.int32, (ROW_BLOCK, width), 0) + i * ROW_BLOCK
            fold_block(
                rows, scale, q_ref, m_ref, acc_ref, nk_ref[:width, :], nv_ref[:width, :], key_at <= row_at
            )

    for rows in parts:
        total = acc_ref[rows, HEAD_DIM:]
        seen = total > 0.0
        safe = jnp.where(seen, total, 1.0)
        o_ref[rows, :] = (acc_ref[rows, :HEAD_DIM] / safe).astype(jnp.bfloat16)
        lse = jnp.where(seen, m_ref[rows, :] * scale + jnp.log2(safe), LOWEST)
        lane = lax.broadcasted_iota(jnp.int32, (ROW_BLOCK, HEAD_DIM), 1)
        before = jnp.where(head == 0, 0.0, lse_ref[rows, :])
        lse_ref[rows, :] = jnp.where(lane == head, lse, before)


def attend(count, queries, cache, new_keys=None, new_values=None):
    span, width = queries.shape
    heads = width // HEAD_DIM
    rows = cache.shape[-2]
    causal = new_keys is not None
    by_head = pl.BlockSpec((span, HEAD_DIM), lambda h, n: (0, h))
    lead = cache.ndim - 3
    shape = (1,) * (lead + 1) + (rows, HEAD_DIM)

    def half(which):
        return pl.BlockSpec(shape, lambda h, n: (0,) * lead + (which, 0, h))

    keys_seen = rows + (span // 2 if causal else 0)
    return pl.pallas_call(
        functools.partial(attend_kernel, causal),
        grid_spec=pltpu.PrefetchScalarGridSpec(
            num_scalar_prefetch=1,
            grid=(heads,),
            in_specs=[by_head, half(0), half(1)] + [by_head] * (2 if causal else 0),
            out_specs=[by_head, pl.BlockSpec((span, HEAD_DIM), lambda h, n: (0, 0))],
            scratch_shapes=[
                pltpu.VMEM((span, HEAD_DIM), jnp.float32),
                pltpu.VMEM((span, 2 * HEAD_DIM), jnp.float32),
            ],
        ),
        out_shape=[
            jax.ShapeDtypeStruct((span, width), jnp.bfloat16),
            jax.ShapeDtypeStruct((span, HEAD_DIM), jnp.float32),
        ],
        compiler_params=params(),
        cost_estimate=pl.CostEstimate(
            flops=8 * span * keys_seen * width,
            bytes_accessed=4 * rows * width + 4 * span * width,
            transcendentals=span * keys_seen * heads,
        ),
        name="attend_own" if causal else "attend_guest",
    )(count, queries, cache, cache, *((new_keys, new_values) if causal else ()))


def merge_kernel(groups, heads, inverse_ref, own_ref, guest_ref, own_lse_ref, guest_lse_ref, w_ref, out_ref, att_ref):
    piece = own_ref.shape[1]

    @pl.when(pl.program_id(0) == 0)
    def _():
        def one_request(request, carry):
            source = inverse_ref[request]
            helper = lax.rem(source + groups // 2, groups)
            own_lse = own_lse_ref[source]
            guest_lse = guest_lse_ref[helper]
            top = jnp.maximum(own_lse, guest_lse)
            own_share = jnp.exp2(own_lse - top)
            guest_share = jnp.exp2(guest_lse - top)
            total = own_share + guest_share
            own_share = own_share / total
            guest_share = guest_share / total
            rows = pl.ds(pl.multiple_of(request * piece, piece), piece)
            for head in range(heads):
                cut = slice(head * HEAD_DIM, (head + 1) * HEAD_DIM)
                merged = own_ref[source, :, cut].astype(jnp.float32) * own_share[
                    :, head : head + 1
                ] + guest_ref[helper, :, cut].astype(jnp.float32) * guest_share[:, head : head + 1]
                att_ref[rows, cut] = merged.astype(jnp.bfloat16)
            return carry

        lax.fori_loop(0, groups, one_request, 0)

    out_ref[...] = jnp.dot(
        att_ref[...], w_ref[...], preferred_element_type=jnp.float32
    ).astype(jnp.bfloat16)


def merge(inverse, own, guest, own_lse, guest_lse, w_out):
    groups, piece, width = own.shape
    heads = width // HEAD_DIM
    columns = w_out.shape[1]
    block = 256
    parts = pl.BlockSpec(own.shape, lambda n, i: (0, 0, 0))
    lse = pl.BlockSpec(own_lse.shape, lambda n, i: (0, 0, 0))
    rows = groups * piece
    return pl.pallas_call(
        functools.partial(merge_kernel, groups, heads),
        grid_spec=pltpu.PrefetchScalarGridSpec(
            num_scalar_prefetch=1,
            grid=(columns // block,),
            in_specs=[parts, parts, lse, lse, pl.BlockSpec((width, block), lambda n, i: (0, n))],
            out_specs=pl.BlockSpec((rows, block), lambda n, i: (0, n)),
            scratch_shapes=[pltpu.VMEM((rows, width), jnp.bfloat16)],
        ),
        out_shape=jax.ShapeDtypeStruct((rows, columns), jnp.bfloat16),
        compiler_params=params(),
        cost_estimate=pl.CostEstimate(
            flops=2 * rows * width * columns,
            bytes_accessed=2 * (2 * rows * width + width * columns + rows * columns),
            transcendentals=0,
        ),
        name="merge",
    )(inverse, own, guest, own_lse, guest_lse, w_out)


def exchange(value):
    return lax.all_to_all(value, "grp", split_axis=0, concat_axis=0, tiled=True)


def shards(
    tokens,
    w_query,
    w_key,
    w_value,
    w_out,
    own_cache,
    guest_cache,
    rec_hidden,
    deal_order,
    own_len,
    guest_len,
    rec_index,
):
    groups = lax.axis_size("grp")
    tp_size = lax.axis_size("tp")
    group_id = lax.axis_index("grp")
    tp_id = lax.axis_index("tp")
    partner_id = (group_id + groups // 2) % groups
    width = w_query.shape[1]
    heads = width // HEAD_DIM
    shard_rows = tokens.shape[1]
    span = shard_rows * groups
    piece = shard_rows // tp_size

    if piece % 16 == 0:
        own_rows, guest_rows = deal(tokens, deal_order, tp_id.astype(jnp.int32)[None], piece)
    else:
        mine = lax.dynamic_slice_in_dim(tokens, tp_id * piece, piece, 1)
        normed = layer_norm(mine).astype(jnp.bfloat16)
        own_rows = jnp.take(normed, deal_order, axis=0)
        guest_rows = jnp.roll(own_rows, groups // 2, axis=0)

    def gathered(rows):
        arrived = lax.all_gather(exchange(rows), "tp", axis=0)
        return jnp.transpose(arrived, (1, 0, 2, 3)).reshape(span, -1)

    own_x = gathered(own_rows)
    guest_x = gathered(guest_rows)

    def place(owner, helper):
        return own_len[owner] + guest_len[helper] + jnp.arange(span, dtype=jnp.int32)

    own_tables = rope_tables(place(group_id, partner_id))
    guest_tables = rope_tables(place(partner_id, group_id))
    rec_tables = rope_tables(rec_index[0])

    rec_rows = layer_norm(rec_hidden[0]).astype(jnp.bfloat16)
    rec_keys, rec_values = project(rec_rows, rec_tables, (w_key, w_value), (True, False))
    cache = replace_rows(own_cache, jnp.stack([rec_keys, rec_values]), rec_index)

    queries, new_keys, new_values = project(
        own_x, own_tables, (w_query, w_key, w_value), (True, True, False)
    )
    (guest_queries,) = project(guest_x, guest_tables, (w_query,), (True,))

    own_out, own_lse = attend(own_len[group_id][None], queries, cache, new_keys, new_values)
    guest_out, guest_lse = attend(guest_len[group_id][None], guest_queries, guest_cache)

    def by_row_owner(value):
        return exchange(value.reshape(groups, shard_rows, -1))

    def stats(lse):
        turned = jnp.transpose(lse[:, :heads].reshape(groups, shard_rows, heads), (0, 2, 1))
        return jnp.transpose(exchange(turned), (0, 2, 1))

    inverse = jnp.zeros_like(deal_order).at[deal_order].set(
        jnp.arange(groups, dtype=deal_order.dtype)
    )
    partial = merge(
        inverse, by_row_owner(own_out), by_row_owner(guest_out), stats(own_lse), stats(guest_lse), w_out
    )
    mixed = lax.psum_scatter(partial, "tp", scatter_dimension=1, tiled=True)
    return mixed.reshape(groups, shard_rows, -1)


def solution(mesh):
    return jax.shard_map(
        shards,
        mesh=mesh,
        in_specs=(
            P(None, "grp", None),
            P(None, "tp"),
            P(None, "tp"),
            P(None, "tp"),
            P("tp", None),
            P("grp", None, None, "tp"),
            P("grp", None, None, "tp"),
            P("grp", None, None),
            P(),
            P(),
            P(),
            P("grp", None),
        ),
        out_specs=P(None, "grp", "tp"),
        check_vma=False,
    )
```

time: 725 us -> 534 us (0.74); the launches traced: 714 us -> 533 us
  Pallas kernels: 0 us -> 183 us
  matrix products: 161 us -> 0 us
  waiting for transfers between devices: 271 us -> 127 us
  blocking collectives: 52.9 us -> 170 us
  other arithmetic: 101 us -> 8.59 us
  local copies, waits for them, and re-layouts: 101 us -> 19.4 us
    pallas_call x0 -> x8, Pallas kernels: none -> 183 us  [the longest x2 114 us: attend(): pl.pallas_call(functools.partial(attend_kernel, causal), grid_spec=pltpu....]
    dot_general x24 -> x0, matrix products: 161 us -> none  [the longest x9 79.5 us: absorb(): jnp.einsum('hqk,khd->qhd', expanded.astype(jnp.bfloat16), value_rows, pre...]
    all_to_all x1 -> x2, waiting for transfers between devices: 184 us -> 37.9 us  [exchange(): return lax.all_to_all(value, 'grp', split_axis=0, concat_axis=0, tiled=True)]
    all_to_all x1 -> x4, blocking collectives: 52.9 us -> 170 us  [exchange(): return lax.all_to_all(value, 'grp', split_axis=0, concat_axis=0, tiled=True)]
    reduce_sum x9 -> x0, other arithmetic: 56.9 us -> none  [absorb(): weight_sum = weight_sum * factor + jnp.sum(expanded, axis=-1)]
    ppermute x1 -> x0, waiting for transfers between devices: 35.4 us -> none  [swapped(): return lax.ppermute(value, axis, pairs)]
    scatter x5 -> x1, local copies, waits for them, and re-layouts: 31.5 us -> 0.62 us  [shards(): jnp.zeros_like(deal_order).at[deal_order]]
    all_gather x0 -> x2, waiting for transfers between devices: none -> 29.5 us  [gathered(): arrived = lax.all_gather(exchange(rows), 'tp', axis=0)]
  transfers between devices with their start and end apart: 3 -> 5, of which waited for: 3 -> 3; matrix products, arithmetic and copies ran while one was open for 32% -> 3% of each run, Pallas kernels for 0% -> 19%
where the time goes in v1:
time: 534 us; the launch traced here: 533 us
  Pallas kernels  183 us (34%)
  blocking collectives  170 us (32%)
  waiting for transfers between devices  127 us (24%)
  local copies, waits for them, and re-layouts  19.4 us (4%)
  between operations  15.9 us (3%)
  starting transfers between devices  8.93 us (2%)
  other arithmetic  8.59 us (2%)
    all_to_all x4, blocking collectives, exchange(): return lax.all_to_all(value, 'grp', split_axis=0, concat_axis=0, tiled=True)  170 us
    pallas_call x2, Pallas kernels, attend(): pl.pallas_call(functools.partial(attend_kernel, causal), grid_spec=pltpu....  114 us
    reduce_scatter x1, waiting for transfers between devices, shards(): mixed = lax.psum_scatter(partial, 'tp', scatter_dimension=1, tiled=True)  60 us
    all_to_all x2, waiting for transfers between devices, exchange(): return lax.all_to_all(value, 'grp', split_axis=0, concat_axis=0, tiled=True)  37.9 us
    pallas_call x3, Pallas kernels, project(): pl.pallas_call(functools.partial(project_kernel, turned, block // HEAD_DI...  32.6 us
    all_gather x2, waiting for transfers between devices, gathered(): arrived = lax.all_gather(exchange(rows), 'tp', axis=0)  29.5 us
    pallas_call x1, Pallas kernels, merge(): pl.pallas_call(functools.partial(merge_kernel, groups, heads), grid_spec=...  14.3 us
    pallas_call x1, Pallas kernels, deal(): pl.pallas_call(deal_kernel, grid_spec=pltpu.PrefetchScalarGridSpec(num_sc...  11.4 us
  transfers between devices with their start and end apart: 5, of which 3 were waited for; matrix products, arithmetic and copies ran while one was open for 3% of the time, Pallas kernels for 19%

profile of v1, /device:TPU:0, one launch (start us, length us, event | category | flops | bytes accessed | tf_op | source)
XLA Modules:
  0.0 532.9 jit_solution(14602521511552019727)
XLA Ops:
  6.5 0.7 copy-done.2
  7.2 11.4 %deal.1 = (bf16[16,32,2048]{2,1,0:T(8,128)(2,1)S(1)}, bf16[16,32,2048]{2,1,0:T(8,128)(2,1)}) custom-call(s32[16]{0:T(128)S(1)} %copy-done.2, s32[1]{0:T(128)} %bitcast.tp_ref, bf16[16,64,2048]{2,1,0:T(8,128)(2,1)} %x_ref.1), custom_call_target="tpu_custom_call" | custom-call | tf_op jit(solution)/shard_map/deal/pallas_call | solution.py:55
  18.6 54.6 %all_to_all.30 = bf16[16,32,2048]{2,1,0:T(8,128)(2,1)} all-to-all(bf16[16,32,2048]{2,1,0:T(8,128)(2,1)S(1)} %get-tuple-element.16), channel_id=1, replica_groups=mesh['grp'=16,'tp'=2] {'grp'}, dimensions={0} | all-to-all | bytes 4194304 | tf_op jit(solution)/shard_map/all_to_all | solution.py:312
  73.2 1.5 copy-done.7
  74.7 52.3 %all_to_all.31 = bf16[16,32,2048]{2,1,0:T(8,128)(2,1)} all-to-all(bf16[16,32,2048]{2,1,0:T(8,128)(2,1)S(1)} %copy-done.7), channel_id=1, replica_groups=mesh['grp'=16,'tp'=2] {'grp'}, dimensions={0} | all-to-all | bytes 4194304 | tf_op jit(solution)/shard_map/all_to_all | solution.py:312
  127.1 0.6 copy-done.1
  127.7 0.7 fusion.10
  132.6 5.7 %project.4 = (bf16[256,1024]{1,0:T(8,128)(2,1)S(1)}, bf16[256,1024]{1,0:T(8,128)(2,1)S(1)}) custom-call(bf16[256,2048]{1,0:T(8,128)(2,1)S(1)} %fusion.4.x_ref, f32[256,128]{1,0:T(8,128)S(1)} %get-tuple-element.45.cos_ref, f32[256,128]{1,0:T(8,128)S(1)} %get-tuple-element.46.sin_ref, bf16[2048,1024]{1,0:T(8,128)(2,1)} %refs_0_.4, bf16[2048,1024]{1,0:T(8,128)(2,1)} %refs_1_.3), custom_call_target="tpu_custom_call" | custom-call | flops 2147483648 | bytes 10485760 | tf_op jit(solution)/shard_map/project/pallas_call | solution.py:94
  138.5 10.8 %replace_rows.1.k_ref.v_ref = bf16[2,2048,1024]{2,1,0:T(8,128)(2,1)} custom-call(s32[1,256]{1,0:T(1,128)S(1)} %copy-done.1, bf16[1,2,2048,1024]{3,2,1,0:T(8,128)(2,1)} %cache_ref.1, bf16[2,256,1024]{2,1,0:T(8,128)(2,1)S(1)} %pad_maximum_fusion.fresh_ref), custom_call_target="tpu_custom_call" | custom-call | tf_op jit(solution)/shard_map/replace_rows/pallas_call | solution.py:126
  149.3 3.7 fusion.6
  153.2 1.0 pad_maximum_fusion.1.cos_ref
  154.7 4.7 copy.15
  159.4 29.5 %all-gather.7.cloned.1.call-done = bf16[32,32,2048]{2,1,0:T(8,128)(2,1)} async-done(((bf16[16,32,2048]{2,1,0:T(8,128)(2,1)}), bf16[32,32,2048]{2,1,0:T(8,128)(2,1)}) %all-gather.7.cloned.1.call-update) | async-done | bytes 4194320 | tf_op jit(solution)/shard_map/all_gather | solution.py:349
  188.9 4.7 copy.16
  193.6 8.1 %project.5.q_ref = bf16[1024,1024]{1,0:T(8,128)(2,1)S(1)} custom-call(bf16[1024,2048]{1,0:T(8,128)(2,1)} %bitcast.48, f32[1024,128]{1,0:T(8,128)S(1)} %pad_maximum_fusion.3.cos_ref, f32[1024,128]{1,0:T(8,128)S(1)} %pad_maximum_fusion.4.sin_ref, bf16[2048,1024]{1,0:T(8,128)(2,1)} %refs_0_.5), custom_call_target="tpu_custom_call" | custom-call | flops 4294967296 | bytes 10485760 | tf_op jit(solution)/shard_map/project/pallas_call | solution.py:94
  201.7 1.3 copy-done.4
  203.0 48.3 %attend_guest.1 = (bf16[1024,1024]{1,0:T(8,128)(2,1)S(1)}, f32[1024,128]{1,0:T(8,128)S(1)}) custom-call(s32[1]{0:T(128)} %get-tuple-element.44.count_ref, bf16[1024,1024]{1,0:T(8,128)(2,1)} %copy-done.4, bf16[1,2,2048,1024]{3,2,1,0:T(8,128)(2,1)} %v_ref.1, bf16[1,2,2048,1024]{3,2,1,0:T(8,128)(2,1)} %v_ref.1), custom_call_target="tpu_custom_call" | custom-call | flops 17179869184 | bytes 12582912 | tf_op jit(solution)/shard_map/attend_guest/pallas_call | solution.py:225
  251.5 0.7 reshape.79
  252.2 3.8 all-to-all-start.5
  256.0 1.0 copy-done
  257.0 18.7 %project.3 = (bf16[1024,1024]{1,0:T(8,128)(2,1)S(1)}, bf16[1024,1024]{1,0:T(8,128)(2,1)}, bf16[1024,1024]{1,0:T(8,128)(2,1)}) custom-call(bf16[1024,2048]{1,0:T(8,128)(2,1)} %bitcast.47, f32[1024,128]{1,0:T(8,128)S(1)} %copy-done, f32[1024,128]{1,0:T(8,128)S(1)} %pad_maximum_fusion.2.sin_ref, bf16[2048,1024]{1,0:T(8,128)(2,1)} %refs_0_.5, ...), custom_call_target="tpu_custom_call" | custom-call | flops 12884901888 | bytes 23068672 | tf_op jit(solution)/shard_map/project/pallas_call | solution.py:94
  275.8 1.3 copy-done.5
  277.1 65.2 %attend_own.1 = (bf16[1024,1024]{1,0:T(8,128)(2,1)}, f32[1024,128]{1,0:T(8,128)S(1)}) custom-call(s32[1]{0:T(128)} %get-tuple-element.40.count_ref, bf16[1024,1024]{1,0:T(8,128)(2,1)} %copy-done.5, bf16[2,2048,1024]{2,1,0:T(8,128)(2,1)} %replace_rows.1.k_ref.v_ref, bf16[2,2048,1024]{2,1,0:T(8,128)(2,1)} %replace_rows.1.k_ref.v_ref, ...), custom_call_target="tpu_custom_call" | custom-call | flops 21474836480 | bytes 12582912 | tf_op jit(solution)/shard_map/attend_own/pallas_call | solution.py:225
  342.7 12.5 %all_to_all.32 = f32[16,1,512]{2,1,0:T(1,128)S(1)} all-to-all(f32[16,1,512]{2,1,0:T(1,128)S(1)} %reshape.77), channel_id=1, replica_groups=mesh['grp'=16,'tp'=2] {'grp'}, dimensions={0} | all-to-all | bytes 65536 | tf_op jit(solution)/shard_map/all_to_all | solution.py:312
  355.2 50.6 %all_to_all.33.guest_ref = bf16[16,64,1024]{2,1,0:T(8,128)(2,1)} all-to-all(bf16[16,64,1024]{2,1,0:T(8,128)(2,1)S(1)} %bitcast.38), channel_id=1, replica_groups=mesh['grp'=16,'tp'=2] {'grp'}, dimensions={0} | all-to-all | bytes 4194304 | tf_op jit(solution)/shard_map/all_to_all | solution.py:312
  405.8 5.1 all-to-all-start.1
  410.9 0.6 scatter_custom_fusion.inverse_ref
  412.0 0.7 reduce.2
  413.1 0.7 reduce.1
  414.1 37.8 %all-to-all-done.1.own_ref = bf16[16,64,1024]{2,1,0:T(8,128)(2,1)S(1)} async-done(((bf16[16,64,1024]{2,1,0:T(8,128)(2,1)}), bf16[16,64,1024]{2,1,0:T(8,128)(2,1)S(1)}, u32[]{:S(2)}, u32[]{:S(2)}) %all-to-all-start.1) | async-done | bytes 2097184 | tf_op jit(solution)/shard_map/all_to_all | solution.py:312
  451.9 14.3 %merge.1 = bf16[1024,2048]{1,0:T(8,128)(2,1)} custom-call(s32[16]{0:T(128)S(1)} %scatter_custom_fusion.inverse_ref, bf16[16,64,1024]{2,1,0:T(8,128)(2,1)S(1)} %all-to-all-done.1.own_ref, bf16[16,64,1024]{2,1,0:T(8,128)(2,1)} %all_to_all.33.guest_ref, f32[16,64,8]{2,1,0:T(8,128)S(1)} %bitcast.40, f32[16,64,8]{2,1,0:T(8,128)S(1)} %bitcast.39, ...), custom_call_target="tpu_custom_call" | custom-call | flops 4294967296 | bytes 12582912 | tf_op jit(solution)/shard_map/merge/pallas_call | solution.py:291
  466.3 60.0 %reduce-scatter.2.cloned.1.call-done = bf16[1024,1024]{1,0:T(8,128)(2,1)} async-done(((bf16[1024,2048]{1,0:T(8,128)(2,1)}), bf16[1024,1024]{1,0:T(8,128)(2,1)}) %reduce-scatter.2.cloned.1.call-update) | async-done | bytes 2097168 | tf_op jit(solution)/shard_map/reduce_scatter | solution.py:387
  (47 shorter events, 4.1 us)
Async XLA Ops:
  6.5 148.1 %all-gather.5.cloned.1.call-start = ((), (), s32[]{:S(2)}) async-start(), calls=%async_computation.8 | async-start | bytes 6291456 | tf_op jit(solution)/shard_map/all_gather | solution.py:349
  6.5 0.7 copy-start.2
  73.1 1.6 copy-start.7
  73.2 115.7 %all-gather.7.cloned.1.call-start = ((), (), s32[]{:S(2)}) async-start(), calls=%async_computation.9 | async-start | bytes 6291456 | tf_op jit(solution)/shard_map/all_gather | solution.py:349
  127.0 0.7 copy-start.1
  127.0 0.7 copy-start.8
  127.1 0.7 copy-start.9
  127.1 4.6 copy-start.6
  201.6 1.3 copy-start.4
  252.2 90.4 %all-to-all-start.5 = ((f32[16,1,512]{2,1,0:T(1,128)}), f32[16,1,512]{2,1,0:T(1,128)S(1)}, u32[]{:S(2)}, u32[]{:S(2)}) async-start(f32[16,1,512]{2,1,0:T(1,128)} %reshape.79), calls=%async_computation.5 | async-start | bytes 65536 | tf_op jit(solution)/shard_map/all_to_all | solution.py:312
  256.0 1.0 copy-start
  275.8 1.3 copy-start.5
  405.8 5.1 copy-start.3
  405.8 46.2 %all-to-all-start.1 = ((bf16[16,64,1024]{2,1,0:T(8,128)(2,1)}), bf16[16,64,1024]{2,1,0:T(8,128)(2,1)S(1)}, u32[]{:S(2)}, u32[]{:S(2)}) async-start(bf16[16,64,1024]{2,1,0:T(8,128)(2,1)} %bitcast.9), calls=%async_computation.1 | async-start | bytes 4194304 | tf_op jit(solution)/shard_map/all_to_all | solution.py:312
  410.8 115.5 %reduce-scatter.2.cloned.1.call-start = ((), (), s32[]{:S(2)}) async-start(), calls=%async_computation.7 | async-start | bytes 6291456 | tf_op jit(solution)/shard_map/reduce_scatter | solution.py:387
Sparse Core Ops, SparseCore 0:
  73.3 57.1 all-gather.4
  132.1 56.7 all-gather.6
  466.4 59.8 reduce-scatter.1

commit v2 on v1

v2 whole, which is shorter than its diff:
```python
import functools
import math

import jax
import jax.numpy as jnp
from jax import lax
from jax.experimental import pallas as pl
from jax.experimental.pallas import tpu as pltpu
from jax.sharding import PartitionSpec as P

HEAD_DIM = 128
KEY_BLOCK = 1024
ROW_BLOCK = 256
VMEM_LIMIT = 50 * 1024 * 1024

rope_base = 10000.0
norm_eps = 1e-05
LOG2E = math.log2(math.e)
LOWEST = -1e30


def params():
    return pltpu.CompilerParams(vmem_limit_bytes=VMEM_LIMIT)


def layer_norm(token_rows):
    widened = token_rows.astype(jnp.float32)
    centred = widened - jnp.mean(widened, axis=-1, keepdims=True)
    variance = jnp.mean(centred * centred, axis=-1, keepdims=True)
    return centred * lax.rsqrt(variance + norm_eps)


def rope_tables(positions):
    half_dim = HEAD_DIM // 2
    frequency = jnp.exp(-jnp.log(rope_base) * jnp.arange(half_dim, dtype=jnp.float32) / half_dim)
    angles = positions.astype(jnp.float32)[:, None] * frequency[None, :]
    cosine = jnp.cos(angles)
    sine = jnp.sin(angles)
    return (
        jnp.concatenate([cosine, cosine], axis=-1),
        jnp.concatenate([-sine, sine], axis=-1),
    )


def deal_kernel(order_ref, tp_ref, x_ref, own_ref, guest_ref):
    first = pl.program_id(0) * own_ref.shape[0]
    for at in range(own_ref.shape[0]):
        normed = layer_norm(x_ref[order_ref[first + at]]).astype(jnp.bfloat16)
        own_ref[at] = normed
        guest_ref[at] = normed


def deal(tokens, deal_order, tp_index, piece):
    groups, _, width = tokens.shape
    each = 4
    steps = groups // each
    out = jax.ShapeDtypeStruct((groups, piece, width), jnp.bfloat16)
    return pl.pallas_call(
        deal_kernel,
        grid_spec=pltpu.PrefetchScalarGridSpec(
            num_scalar_prefetch=2,
            grid=(steps,),
            in_specs=[pl.BlockSpec((groups, piece, width), lambda d, order, t: (0, t[0], 0))],
            out_specs=[
                pl.BlockSpec((each, piece, width), lambda d, order, t: (d, 0, 0)),
                pl.BlockSpec(
                    (each, piece, width), lambda d, order, t: ((d + steps // 2) % steps, 0, 0)
                ),
            ],
        ),
        out_shape=[out, out],
        compiler_params=params(),
        name="deal",
    )(deal_order, tp_index, tokens)


def project_kernel(turned, heads, halves, tp_ref, *refs):
    if halves:
        mine_ref, other_ref, cos_ref, sin_ref, *refs, x_ref = refs
        shards_in, piece, _ = mine_ref.shape

        @pl.when(pl.program_id(0) == 0)
        def _():
            t = tp_ref[0]
            for shard in range(shards_in):
                for half_ref, at in ((mine_ref, t), (other_ref, 1 - t)):
                    start = pl.multiple_of((2 * shard + at) * piece, piece)
                    x_ref[pl.ds(start, piece), :] = half_ref[shard]
    else:
        x_ref, cos_ref, sin_ref, *refs = refs
    count = len(turned)
    x = x_ref[...]
    for w_ref, out_ref, turn in zip(refs[:count], refs[count:], turned):
        product = jnp.dot(x, w_ref[...], preferred_element_type=jnp.float32)
        if not turn:
            out_ref[...] = product.astype(jnp.bfloat16)
            continue
        for head in range(heads):
            cut = slice(head * HEAD_DIM, (head + 1) * HEAD_DIM)
            part = product[:, cut]
            swapped = pltpu.roll(part, HEAD_DIM // 2, 1)
            out_ref[:, cut] = (part * cos_ref[...] + swapped * sin_ref[...]).astype(jnp.bfloat16)


def project(x, tp_index, tables, weights, turned):
    depth = x[0].shape[-1]
    rows = math.prod(x[0].shape[:-1]) * len(x)
    width = weights[0].shape[1]
    block = min(256, width)
    halves = len(x) == 2
    table = pl.BlockSpec((rows, HEAD_DIM), lambda n, t: (0, 0))
    count = len(weights)
    return pl.pallas_call(
        functools.partial(project_kernel, turned, block // HEAD_DIM, halves),
        grid_spec=pltpu.PrefetchScalarGridSpec(
            num_scalar_prefetch=1,
            grid=(width // block,),
            in_specs=[pl.BlockSpec(part.shape, lambda n, t, r=part.ndim: (0,) * r) for part in x]
            + [table, table]
            + [pl.BlockSpec((depth, block), lambda n, t: (0, n))] * count,
            out_specs=[pl.BlockSpec((rows, block), lambda n, t: (0, n))] * count,
            scratch_shapes=[pltpu.VMEM((rows, depth), jnp.bfloat16)] if halves else [],
        ),
        out_shape=[jax.ShapeDtypeStruct((rows, width), jnp.bfloat16)] * count,
        compiler_params=params(),
        cost_estimate=pl.CostEstimate(
            flops=2 * rows * depth * width * count,
            bytes_accessed=2 * (rows * depth + count * width * (rows + depth)),
            transcendentals=0,
        ),
        name="project",
    )(tp_index, *x, *tables, *weights)


def replace_kernel(block, index_ref, cache_ref, fresh_ref, out_ref):
    first = pl.program_id(1) * block
    count = index_ref.shape[1]
    row = first + lax.broadcasted_iota(jnp.int32, (block, count), 0)
    hits = jnp.where(row == index_ref[...], 1.0, 0.0)
    picked = jnp.dot(
        hits.astype(jnp.bfloat16), fresh_ref[0], preferred_element_type=jnp.float32
    )
    is_hit = jnp.sum(hits, axis=1, keepdims=True) > 0.5
    out_ref[0] = jnp.where(is_hit, picked, cache_ref[0, 0].astype(jnp.float32)).astype(jnp.bfloat16)


def replace_rows(cache, fresh, rec_index):
    _, _, rows, width = cache.shape
    count = rec_index.shape[1]
    block = 512
    return pl.pallas_call(
        functools.partial(replace_kernel, block),
        grid=(2, rows // block),
        in_specs=[
            pl.BlockSpec((1, count), lambda c, r: (0, 0)),
            pl.BlockSpec((1, 1, block, width), lambda c, r: (0, c, r, 0)),
            pl.BlockSpec((1, count, width), lambda c, r: (c, 0, 0)),
        ],
        out_specs=pl.BlockSpec((1, block, width), lambda c, r: (c, r, 0)),
        out_shape=jax.ShapeDtypeStruct((2, rows, width), jnp.bfloat16),
        compiler_params=params(),
        cost_estimate=pl.CostEstimate(
            flops=4 * rows * count * width, bytes_accessed=10 * rows * width, transcendentals=0
        ),
        name="replace_rows",
    )(rec_index, cache, fresh)


def fold_keys(jobs, q_ref, m_ref, acc_ref):
    scale = HEAD_DIM**-0.5 * LOG2E

    def scores_of(job):
        rows, keys, _, mask = job
        scores = lax.dot_general(
            q_ref[rows, :], keys(), (((1,), (1,)), ((), ())), preferred_element_type=jnp.float32
        )
        return scores if mask is None else jnp.where(mask, scores, LOWEST)

    upcoming = scores_of(jobs[0])
    for at, (rows, _, values, _) in enumerate(jobs):
        scores = upcoming
        if at + 1 < len(jobs):
            upcoming = scores_of(jobs[at + 1])
        old_max = m_ref[rows, :]
        new_max = jnp.maximum(old_max, jnp.max(scores, axis=1, keepdims=True))
        factor = jnp.exp2((old_max - new_max) * scale)
        shift = new_max * scale
        tiles = scores.shape[1] // HEAD_DIM
        weights = jnp.exp2(scores * scale - jnp.concatenate([shift] * tiles, axis=1))
        seen = values()
        widened = jnp.concatenate([seen, jnp.ones(seen.shape, jnp.bfloat16)], axis=1)
        product = jnp.dot(
            weights.astype(jnp.bfloat16), widened, preferred_element_type=jnp.float32
        )
        acc_ref[rows, :] = acc_ref[rows, :] * jnp.concatenate([factor, factor], axis=1) + product
        m_ref[rows, :] = new_max


def attend_kernel(causal, chunks, count_ref, q_ref, k_ref, v_ref, *refs):
    if causal:
        nk_ref, nv_ref, *refs = refs
    *o_refs, lse_ref, m_ref, acc_ref = refs
    scale = HEAD_DIM**-0.5 * LOG2E
    span = q_ref.shape[0]
    used = count_ref[0]
    parts = [pl.ds(i * ROW_BLOCK, ROW_BLOCK) for i in range(span // ROW_BLOCK)]
    m_ref[...] = jnp.full(m_ref.shape, LOWEST, jnp.float32)
    acc_ref[...] = jnp.zeros(acc_ref.shape, jnp.float32)
    k_all = k_ref.at[(0,) * (len(k_ref.shape) - 2)]
    v_all = v_ref.at[(0,) * (len(v_ref.shape) - 2)]

    def visit(block, masked):
        start = pl.multiple_of(block * KEY_BLOCK, KEY_BLOCK)
        mask = None
        if masked:
            place = lax.broadcasted_iota(jnp.int32, (1, KEY_BLOCK), 1)
            mask = place < used - start
        picked = pl.ds(start, KEY_BLOCK)
        jobs = [(rows, lambda: k_all[picked, :], lambda: v_all[picked, :], mask) for rows in parts]
        fold_keys(jobs, q_ref, m_ref, acc_ref)

    full = used // KEY_BLOCK
    pl.loop(0, full)(lambda block: visit(block, False))

    @pl.when(used % KEY_BLOCK > 0)
    def _():
        visit(full, True)

    if causal:
        jobs = []
        for i, rows in enumerate(parts):
            width = (i + 1) * ROW_BLOCK
            key_at = lax.broadcasted_iota(jnp.int32, (ROW_BLOCK, width), 1)
            row_at = lax.broadcasted_iota(jnp.int32, (ROW_BLOCK, width), 0) + i * ROW_BLOCK
            jobs.append(
                (
                    rows,
                    lambda width=width: nk_ref[:width, :],
                    lambda width=width: nv_ref[:width, :],
                    key_at <= row_at,
                )
            )
        fold_keys(jobs, q_ref, m_ref, acc_ref)

    shard_rows = o_refs[0].shape[1] * chunks
    piece = shard_rows // chunks
    for i, rows in enumerate(parts):
        total = acc_ref[rows, HEAD_DIM:]
        seen = total > 0.0
        safe = jnp.where(seen, total, 1.0)
        out = (acc_ref[rows, :HEAD_DIM] / safe).astype(jnp.bfloat16)
        for at in range(0, ROW_BLOCK, piece):
            shard, chunk = divmod(i * ROW_BLOCK + at, shard_rows)
            o_refs[chunk // piece][shard] = out[at : at + piece, :]
        lse = jnp.where(seen, m_ref[rows, :] * scale + jnp.log2(safe), LOWEST)
        lse_ref[0, :, rows] = jnp.transpose(lse)[:1, :]


def attend(count, groups, chunks, queries, cache, new_keys=None, new_values=None):
    span, width = queries.shape
    heads = width // HEAD_DIM
    rows = cache.shape[-2]
    causal = new_keys is not None
    by_head = pl.BlockSpec((span, HEAD_DIM), lambda h, n: (0, h))
    lead = cache.ndim - 3
    shape = (1,) * (lead + 1) + (rows, HEAD_DIM)
    piece = span // groups // chunks

    def half(which):
        return pl.BlockSpec(shape, lambda h, n: (0,) * lead + (which, 0, h))

    keys_seen = rows + (span // 2 if causal else 0)
    return pl.pallas_call(
        functools.partial(attend_kernel, causal, chunks),
        grid_spec=pltpu.PrefetchScalarGridSpec(
            num_scalar_prefetch=1,
            grid=(heads,),
            in_specs=[by_head, half(0), half(1)] + [by_head] * (2 if causal else 0),
            out_specs=[pl.BlockSpec((groups, piece, HEAD_DIM), lambda h, n: (0, 0, h))] * chunks
            + [pl.BlockSpec((1, 1, span), lambda h, n: (h, 0, 0))],
            scratch_shapes=[
                pltpu.VMEM((span, HEAD_DIM), jnp.float32),
                pltpu.VMEM((span, 2 * HEAD_DIM), jnp.float32),
            ],
        ),
        out_shape=[jax.ShapeDtypeStruct((groups, piece, width), jnp.bfloat16)] * chunks
        + [jax.ShapeDtypeStruct((heads, 1, span), jnp.float32)],
        compiler_params=params(),
        cost_estimate=pl.CostEstimate(
            flops=16 * span * keys_seen * width,
            bytes_accessed=4 * rows * width + 4 * span * width,
            transcendentals=span * keys_seen * heads,
        ),
        name="attend_own" if causal else "attend_guest",
    )(count, queries, cache, cache, *((new_keys, new_values) if causal else ()))


def merge_kernel(groups, heads, inverse_ref, own_ref, guest_ref, own_lse_ref, guest_lse_ref, w_ref, out_ref, att_ref):
    piece = own_ref.shape[1]

    @pl.when(pl.program_id(0) == 0)
    def _():
        def one_request(request, carry):
            source = inverse_ref[request]
            helper = lax.rem(source + groups // 2, groups)
            own_lse = own_lse_ref[source]
            guest_lse = guest_lse_ref[helper]
            top = jnp.maximum(own_lse, guest_lse)
            own_share = jnp.exp2(own_lse - top)
            guest_share = jnp.exp2(guest_lse - top)
            total = own_share + guest_share
            own_share = own_share / total
            guest_share = guest_share / total
            rows = pl.ds(pl.multiple_of(request * piece, piece), piece)
            for head in range(heads):
                cut = slice(head * HEAD_DIM, (head + 1) * HEAD_DIM)
                merged = own_ref[source, :, cut].astype(jnp.float32) * own_share[
                    :, head : head + 1
                ] + guest_ref[helper, :, cut].astype(jnp.float32) * guest_share[:, head : head + 1]
                att_ref[rows, cut] = merged.astype(jnp.bfloat16)
            return carry

        lax.fori_loop(0, groups, one_request, 0)

    out_ref[...] = jnp.dot(
        att_ref[...], w_ref[...], preferred_element_type=jnp.float32
    ).astype(jnp.bfloat16)


def merge(inverse, chunk, own, guest, own_lse, guest_lse, w_out):
    groups, piece, width = guest.shape
    heads = width // HEAD_DIM
    columns = w_out.shape[1]
    block = 512
    rows = groups * piece

    def part(last):
        return pl.BlockSpec((groups, piece, last), lambda n, i: (0, chunk, 0))

    return pl.pallas_call(
        functools.partial(merge_kernel, groups, heads),
        grid_spec=pltpu.PrefetchScalarGridSpec(
            num_scalar_prefetch=1,
            grid=(columns // block,),
            in_specs=[
                part(width),
                pl.BlockSpec(guest.shape, lambda n, i: (0, 0, 0)),
                part(heads),
                part(heads),
                pl.BlockSpec((width, block), lambda n, i: (0, n)),
            ],
            out_specs=pl.BlockSpec((rows, block), lambda n, i: (0, n)),
            scratch_shapes=[pltpu.VMEM((rows, width), jnp.bfloat16)],
        ),
        out_shape=jax.ShapeDtypeStruct((rows, columns), jnp.bfloat16),
        compiler_params=params(),
        cost_estimate=pl.CostEstimate(
            flops=4 * rows * width * columns,
            bytes_accessed=2 * (2 * rows * width + width * columns + rows * columns),
            transcendentals=0,
        ),
        name="merge",
    )(inverse, own, guest, own_lse, guest_lse, w_out)


def exchange(value):
    return lax.all_to_all(value, "grp", split_axis=0, concat_axis=0, tiled=True)


def shards(
    tokens,
    w_query,
    w_key,
    w_value,
    w_out,
    own_cache,
    guest_cache,
    rec_hidden,
    deal_order,
    own_len,
    guest_len,
    rec_index,
):
    groups = lax.axis_size("grp")
    tp_size = lax.axis_size("tp")
    group_id = lax.axis_index("grp")
    tp_id = lax.axis_index("tp")
    partner_id = (group_id + groups // 2) % groups
    width = w_query.shape[1]
    heads = width // HEAD_DIM
    shard_rows = tokens.shape[1]
    span = shard_rows * groups
    piece = shard_rows // tp_size

    chunks = 2
    tp_index = tp_id.astype(jnp.int32)[None]
    tied = lax.optimization_barrier

    if piece % 16 == 0:
        own_rows, guest_rows = deal(tokens, deal_order, tp_index, piece)
    else:
        mine = lax.dynamic_slice_in_dim(tokens, tp_id * piece, piece, 1)
        normed = layer_norm(mine).astype(jnp.bfloat16)
        own_rows = jnp.take(normed, deal_order, axis=0)
        guest_rows = jnp.roll(own_rows, groups // 2, axis=0)

    def gathered(arrived):
        if tp_size == 2 and piece % 16 == 0:
            return (arrived, lax.ppermute(arrived, "tp", [(0, 1), (1, 0)]))
        arrived = lax.all_gather(arrived, "tp", axis=0)
        return (jnp.transpose(arrived, (1, 0, 2, 3)).reshape(span, -1),)

    def place(owner, helper):
        return own_len[owner] + guest_len[helper] + jnp.arange(span, dtype=jnp.int32)

    own_arrived = exchange(own_rows)
    own_tables = rope_tables(place(group_id, partner_id))
    guest_tables = rope_tables(place(partner_id, group_id))
    rec_tables = rope_tables(rec_index[0])
    rec_rows = layer_norm(rec_hidden[0]).astype(jnp.bfloat16)
    rec_keys, rec_values = project((rec_rows,), tp_index, rec_tables, (w_key, w_value), (True, False))
    cache = replace_rows(own_cache, jnp.stack([rec_keys, rec_values]), rec_index)
    cache, own_tables, guest_tables, own_arrived, guest_rows = tied(
        (cache, own_tables, guest_tables, own_arrived, guest_rows)
    )

    own_x = gathered(own_arrived)
    guest_arrived = exchange(guest_rows)
    queries, new_keys, new_values = project(
        own_x, tp_index, own_tables, (w_query, w_key, w_value), (True, True, False)
    )
    guest_arrived, queries = tied((guest_arrived, queries))
    guest_x = gathered(guest_arrived)
    own_out, own_lse = attend(
        own_len[group_id][None], groups, 1, queries, cache, new_keys, new_values
    )
    guest_x, own_out = tied((guest_x, own_out))

    own_part = exchange(own_out)
    (guest_queries,) = project(guest_x, tp_index, guest_tables, (w_query,), (True,))
    *guest_out, guest_lse = attend(
        guest_len[group_id][None], groups, chunks, guest_queries, guest_cache
    )
    stats = lax.all_gather(jnp.concatenate([own_lse, guest_lse])[:, 0], "grp", axis=0)
    stats = lax.dynamic_slice_in_dim(stats, group_id * shard_rows, shard_rows, 2)
    stats = jnp.transpose(stats, (0, 2, 1))
    own_stats, guest_stats = stats[..., :heads], stats[..., heads:]

    inverse = jnp.sum(
        jnp.where(
            deal_order[None, :] == jnp.arange(groups, dtype=deal_order.dtype)[:, None],
            jnp.arange(groups, dtype=jnp.int32)[None, :],
            0,
        ),
        axis=1,
    )
    mixed = []
    for chunk in range(chunks):
        guest_part = exchange(guest_out[chunk])
        if chunk + 1 < chunks:
            guest_part, guest_out[chunk + 1] = tied((guest_part, guest_out[chunk + 1]))
        partial = merge(inverse, chunk, own_part, guest_part, own_stats, guest_stats, w_out)
        summed = lax.psum_scatter(partial, "tp", scatter_dimension=1, tiled=True)
        mixed.append(summed.reshape(groups, shard_rows // chunks, -1))
    return jnp.concatenate(mixed, axis=1)


def solution(mesh):
    return jax.shard_map(
        shards,
        mesh=mesh,
        in_specs=(
            P(None, "grp", None),
            P(None, "tp"),
            P(None, "tp"),
            P(None, "tp"),
            P("tp", None),
            P("grp", None, None, "tp"),
            P("grp", None, None, "tp"),
            P("grp", None, None),
            P(),
            P(),
            P(),
            P("grp", None),
        ),
        out_specs=P(None, "grp", "tp"),
        check_vma=False,
    )
```

time: 534 us -> 416 us (0.78)
  blocking collectives: 170 us -> 56.9 us
  Pallas kernels: 183 us -> 136 us
  waiting for transfers between devices: 127 us -> 158 us
  starting transfers between devices: 8.93 us -> 27.2 us
  local copies, waits for them, and re-layouts: 19.4 us -> 11.2 us
    all_to_all x4 -> x2, blocking collectives: 170 us -> 56.9 us  [exchange(): return lax.all_to_all(value, 'grp', split_axis=0, concat_axis=0, tiled=True)]
    ppermute x0 -> x2, waiting for transfers between devices: none -> 53.5 us  [gathered(): return (arrived, lax.ppermute(arrived, 'tp', [(0, 1), (1, 0)]))]
    pallas_call x2, Pallas kernels: 114 us -> 67.8 us  [attend(): pl.pallas_call(functools.partial(attend_kernel, causal, chunks), grid_spe...]
    reduce_scatter x1 -> x2, waiting for transfers between devices: 60 us -> 32 us  [shards(): summed = lax.psum_scatter(partial, 'tp', scatter_dimension=1, tiled=True)]
    all_gather x2 -> x1, waiting for transfers between devices: 29.5 us -> 57.5 us  [shards(): lax.all_gather(jnp.concatenate([own_lse, guest_lse])[:, 0], 'grp', axis=0)]
    all_to_all x2 -> x3, waiting for transfers between devices: 37.9 us -> 14.9 us  [exchange(): return lax.all_to_all(value, 'grp', split_axis=0, concat_axis=0, tiled=True)]
    all_to_all x2 -> x3, starting transfers between devices: 8.85 us -> 24 us  [exchange(): return lax.all_to_all(value, 'grp', split_axis=0, concat_axis=0, tiled=True)]
    all_gather x2 -> x0, local copies, waits for them, and re-layouts: 9.42 us -> none  [gathered(): arrived = lax.all_gather(exchange(rows), 'tp', axis=0)]
  transfers between devices with their start and end apart: 5 -> 8, of which waited for: 3 -> 5; matrix products, arithmetic and copies ran while one was open for 3% -> 3% of each run, Pallas kernels for 19% -> 20%
where the time goes in v2:
time: 416 us; the launch traced here: 415 us
  waiting for transfers between devices  158 us (38%)
  Pallas kernels  136 us (33%)
  blocking collectives  56.9 us (14%)
  starting transfers between devices  27.2 us (7%)
  between operations  15.7 us (4%)
  local copies, waits for them, and re-layouts  11.2 us (3%)
  other arithmetic  10.1 us (2%)
    pallas_call x2, Pallas kernels, attend(): pl.pallas_call(functools.partial(attend_kernel, causal, chunks), grid_spe...  67.8 us
    all_gather x1, waiting for transfers between devices, shards(): lax.all_gather(jnp.concatenate([own_lse, guest_lse])[:, 0], 'grp', axis=0)  57.5 us
    all_to_all x2, blocking collectives, exchange(): return lax.all_to_all(value, 'grp', split_axis=0, concat_axis=0, tiled=True)  56.9 us
    ppermute x2, waiting for transfers between devices, gathered(): return (arrived, lax.ppermute(arrived, 'tp', [(0, 1), (1, 0)]))  53.5 us
    pallas_call x3, Pallas kernels, project(): pl.pallas_call(functools.partial(project_kernel, turned, block // HEAD_DI...  33.6 us
    reduce_scatter x2, waiting for transfers between devices, shards(): summed = lax.psum_scatter(partial, 'tp', scatter_dimension=1, tiled=True)  32 us
    all_to_all x3, starting transfers between devices, exchange(): return lax.all_to_all(value, 'grp', split_axis=0, concat_axis=0, tiled=True)  24 us
    pallas_call x2, Pallas kernels, merge(): pl.pallas_call(functools.partial(merge_kernel, groups, heads), grid_spec=...  18.5 us
  transfers between devices with their start and end apart: 8, of which 5 were waited for; matrix products, arithmetic and copies ran while one was open for 3% of the time, Pallas kernels for 20%

profile of v2, /device:TPU:0, one launch (start us, length us, event | category | flops | bytes accessed | tf_op | source)
XLA Modules:
  0.0 414.9 jit_solution(5216306205440238099)
XLA Ops:
  6.5 0.7 copy-done.1
  7.2 5.2 %deal.1 = (bf16[16,32,2048]{2,1,0:T(8,128)(2,1)}, bf16[16,32,2048]{2,1,0:T(8,128)(2,1)}) custom-call(s32[16]{0:T(128)S(1)} %copy-done.1, s32[1]{0:T(128)} %bitcast.tp_ref, bf16[16,64,2048]{2,1,0:T(8,128)(2,1)} %x_ref.1), custom_call_target="tpu_custom_call" | custom-call | tf_op jit(solution)/shard_map/deal/pallas_call | solution.py:58
  12.5 7.6 %all-to-all-start = ((bf16[16,32,2048]{2,1,0:T(8,128)(2,1)}), bf16[16,32,2048]{2,1,0:T(8,128)(2,1)}, u32[]{:S(2)}, u32[]{:S(2)}) async-start(bf16[16,32,2048]{2,1,0:T(8,128)(2,1)} %get-tuple-element.33), calls=%async_computation | async-start | bytes 4194304 | tf_op jit(solution)/shard_map/all_to_all | solution.py:367
  25.4 5.7 %project.3 = (bf16[256,1024]{1,0:T(8,128)(2,1)S(1)}, bf16[256,1024]{1,0:T(8,128)(2,1)S(1)}) custom-call(s32[1]{0:T(128)} %bitcast.tp_ref, bf16[256,2048]{1,0:T(8,128)(2,1)S(1)} %fusion.4.refs_0_, f32[256,128]{1,0:T(8,128)S(1)} %get-tuple-element.75.refs_1_, f32[256,128]{1,0:T(8,128)S(1)} %get-tuple-element.76.refs_2_, bf16[2048,1024]{1,0:T(8,128)(2,1)} %refs_5_.1, ...), custom_call_target="tpu_custom_call" | custom-call | flops 2147483648 | bytes 10485760 | tf_op jit(solution)/shard_map/project/pallas_call | solution.py:113
  31.3 3.7 fusion.6
  35.7 10.6 %replace_rows.1.k_ref.v_ref = bf16[2,2048,1024]{2,1,0:T(8,128)(2,1)} custom-call(s32[1,256]{1,0:T(1,128)S(1)} %copy-done, bf16[1,2,2048,1024]{3,2,1,0:T(8,128)(2,1)} %cache_ref.1, bf16[2,256,1024]{2,1,0:T(8,128)(2,1)S(1)} %pad_maximum_fusion.1.fresh_ref), custom_call_target="tpu_custom_call" | custom-call | flops 2147483648 | bytes 20971520 | tf_op jit(solution)/shard_map/replace_rows/pallas_call | solution.py:151
  46.3 14.9 %all-to-all-done.refs_0_ = bf16[16,32,2048]{2,1,0:T(8,128)(2,1)} async-done(((bf16[16,32,2048]{2,1,0:T(8,128)(2,1)}), bf16[16,32,2048]{2,1,0:T(8,128)(2,1)}, u32[]{:S(2)}, u32[]{:S(2)}) %all-to-all-start) | async-done | bytes 2097184 | tf_op jit(solution)/shard_map/all_to_all | solution.py:367
  61.2 11.3 %all-to-all-start.1 = ((bf16[16,32,2048]{2,1,0:T(8,128)(2,1)}), bf16[16,32,2048]{2,1,0:T(8,128)(2,1)}, u32[]{:S(2)}, u32[]{:S(2)}) async-start(bf16[16,32,2048]{2,1,0:T(8,128)(2,1)} %get-tuple-element.35), calls=%async_computation.1 | async-start | bytes 4194304 | tf_op jit(solution)/shard_map/all_to_all | solution.py:367
  72.5 1.6 collective-permute-start
  74.0 46.6 %collective-permute-done.refs_1_ = bf16[16,32,2048]{2,1,0:T(8,128)(2,1)S(1)} collective-permute-done((bf16[16,32,2048]{2,1,0:T(8,128)(2,1)}, bf16[16,32,2048]{2,1,0:T(8,128)(2,1)S(1)}, u32[]{:S(2)}, u32[]{:S(2)}) %collective-permute-start) | collective-permute-done | bytes 2097184 | tf_op jit(solution)/shard_map/ppermute | solution.py:409
  120.6 1.3 copy-done.9
  121.9 19.4 %project.4 = (bf16[1024,1024]{1,0:T(8,128)(2,1)S(1)}, bf16[1024,1024]{1,0:T(8,128)(2,1)}, bf16[1024,1024]{1,0:T(8,128)(2,1)}) custom-call(s32[1]{0:T(128)} %bitcast.tp_ref, bf16[16,32,2048]{2,1,0:T(8,128)(2,1)} %all-to-all-done.refs_0_, bf16[16,32,2048]{2,1,0:T(8,128)(2,1)} %copy-done.9, f32[1024,128]{1,0:T(8,128)S(1)} %get-tuple-element.37.refs_2_, ...), custom_call_target="tpu_custom_call" | custom-call | flops 12884901888 | bytes 23068672 | tf_op jit(solution)/shard_map/project/pallas_call | solution.py:113
  141.3 1.3 copy-done.4
  142.6 1.5 collective-permute-start.1
  144.1 38.8 %attend_own.1 = (bf16[16,64,1024]{2,1,0:T(8,128)(2,1)}, f32[8,1,1024]{2,1,0:T(1,128)S(1)}) custom-call(s32[1]{0:T(128)} %get-tuple-element.74.count_ref, bf16[1024,1024]{1,0:T(8,128)(2,1)} %copy-done.4, bf16[2,2048,1024]{2,1,0:T(8,128)(2,1)} %replace_rows.1.k_ref.v_ref, bf16[2,2048,1024]{2,1,0:T(8,128)(2,1)} %replace_rows.1.k_ref.v_ref, ...), custom_call_target="tpu_custom_call" | custom-call | flops 42949672960 | bytes 12582912 | tf_op jit(solution)/shard_map/attend_own/pallas_call | solution.py:273
  183.0 6.9 %collective-permute-done.1.refs_1_ = bf16[16,32,2048]{2,1,0:T(8,128)(2,1)S(1)} collective-permute-done((bf16[16,32,2048]{2,1,0:T(8,128)(2,1)}, bf16[16,32,2048]{2,1,0:T(8,128)(2,1)S(1)}, u32[]{:S(2)}, u32[]{:S(2)}) %collective-permute-start.1) | collective-permute-done | bytes 2097184 | tf_op jit(solution)/shard_map/ppermute | solution.py:409
  189.9 1.3 copy-done.8
  191.2 8.5 %project.5.q_ref = bf16[1024,1024]{1,0:T(8,128)(2,1)S(1)} custom-call(s32[1]{0:T(128)} %bitcast.tp_ref, bf16[16,32,2048]{2,1,0:T(8,128)(2,1)} %all-to-all-done.1.refs_0_, bf16[16,32,2048]{2,1,0:T(8,128)(2,1)} %copy-done.8, f32[1024,128]{1,0:T(8,128)S(1)} %get-tuple-element.49.refs_2_, f32[1024,128]{1,0:T(8,128)S(1)} %get-tuple-element.50.refs_3_, ...), custom_call_target="tpu_custom_call" | custom-call | flops 4294967296 | bytes 10485760 | tf_op jit(solution)/shard_map/project/pallas_call | solution.py:113
  199.8 1.3 copy-done.3
  201.1 29.0 %attend_guest.1 = (bf16[16,32,1024]{2,1,0:T(8,128)(2,1)S(1)}, bf16[16,32,1024]{2,1,0:T(8,128)(2,1)S(1)}, f32[8,1,1024]{2,1,0:T(1,128)S(1)}) custom-call(s32[1]{0:T(128)} %get-tuple-element.71.count_ref, bf16[1024,1024]{1,0:T(8,128)(2,1)} %copy-done.3, bf16[1,2,2048,1024]{3,2,1,0:T(8,128)(2,1)} %v_ref.1, bf16[1,2,2048,1024]{3,2,1,0:T(8,128)(2,1)} %v_ref.1), custom_call_target="tpu_custom_call" | custom-call | flops 34359738368 | bytes 12582912 | tf_op jit(solution)/shard_map/attend_guest/pallas_call | solution.py:273
  230.1 28.7 %all_to_all.25.guest_ref = bf16[16,32,1024]{2,1,0:T(8,128)(2,1)S(1)} all-to-all(bf16[16,32,1024]{2,1,0:T(8,128)(2,1)S(1)} %get-tuple-element.51), channel_id=1, replica_groups=mesh['grp'=16,'tp'=2] {'grp'}, dimensions={0} | all-to-all | bytes 2097152 | tf_op jit(solution)/shard_map/all_to_all | solution.py:367
  258.8 5.2 %all-to-all-start.2 = ((bf16[16,64,1024]{2,1,0:T(8,128)(2,1)}), bf16[16,64,1024]{2,1,0:T(8,128)(2,1)}, u32[]{:S(2)}, u32[]{:S(2)}) async-start(bf16[16,64,1024]{2,1,0:T(8,128)(2,1)} %get-tuple-element.46), calls=%async_computation.2 | async-start | bytes 4194304 | tf_op jit(solution)/shard_map/all_to_all | solution.py:367
  264.0 0.7 pad_maximum_fusion.8
  264.9 57.5 %all-gather.3.cloned.1.call-done = f32[256,1,1024]{2,1,0:T(1,128)} async-done(((f32[16,1,1024]{2,1,0:T(1,128)}), f32[256,1,1024]{2,1,0:T(1,128)}) %all-gather.3.cloned.1.call-update) | async-done | bytes 1048592 | tf_op jit(solution)/shard_map/all_gather | solution.py:444
  322.3 1.4 copy.16
  323.9 1.0 copy.17
  324.9 1.5 fusion.8
  326.4 9.3 %merge.2 = bf16[512,2048]{1,0:T(8,128)(2,1)} custom-call(s32[16]{0:T(128)S(1)} %select_reduce_fusion.inverse_ref, bf16[16,64,1024]{2,1,0:T(8,128)(2,1)} %all-to-all-done.2.own_ref, bf16[16,32,1024]{2,1,0:T(8,128)(2,1)S(1)} %all_to_all.25.guest_ref, f32[16,64,8]{2,1,0:T(8,128)S(1)} %get-tuple-element.58.own_lse_ref, ...), custom_call_target="tpu_custom_call" | custom-call | flops 4294967296 | bytes 8388608 | tf_op jit(solution)/shard_map/merge/pallas_call | solution.py:340
  335.7 28.2 %all_to_all.26.guest_ref = bf16[16,32,1024]{2,1,0:T(8,128)(2,1)S(1)} all-to-all(bf16[16,32,1024]{2,1,0:T(8,128)(2,1)S(1)} %get-tuple-element.56), channel_id=1, replica_groups=mesh['grp'=16,'tp'=2] {'grp'}, dimensions={0} | all-to-all | bytes 2097152 | tf_op jit(solution)/shard_map/all_to_all | solution.py:367
  364.0 9.2 %merge.3 = bf16[512,2048]{1,0:T(8,128)(2,1)} custom-call(s32[16]{0:T(128)S(1)} %select_reduce_fusion.inverse_ref, bf16[16,64,1024]{2,1,0:T(8,128)(2,1)} %all-to-all-done.2.own_ref, bf16[16,32,1024]{2,1,0:T(8,128)(2,1)S(1)} %all_to_all.26.guest_ref, f32[16,64,8]{2,1,0:T(8,128)S(1)} %get-tuple-element.58.own_lse_ref, ...), custom_call_target="tpu_custom_call" | custom-call | flops 4294967296 | bytes 8388608 | tf_op jit(solution)/shard_map/merge/pallas_call | solution.py:340
  373.3 32.0 %reduce-scatter.5.cloned.1.call-done = bf16[512,1024]{1,0:T(8,128)(2,1)} async-done(((bf16[512,2048]{1,0:T(8,128)(2,1)}), bf16[512,1024]{1,0:T(8,128)(2,1)}) %reduce-scatter.5.cloned.1.call-update) | async-done | bytes 1048592 | tf_op jit(solution)/shard_map/reduce_scatter | solution.py:463
  405.3 3.1 pad_maximum_fusion
  (42 shorter events, 4.1 us)
Async XLA Ops:
  6.5 0.7 copy-start.1
  12.4 7.6 %copy-start = (s32[1,256]{1,0:T(1,128)S(1)}, s32[1,256]{1,0:T(1,128)}, u32[]{:S(2)}) copy-start(s32[1,256]{1,0:T(1,128)} %index_ref.1) | copy-start | bytes 3076
  12.4 7.6 %copy-start.6 = (s32[16]{0:T(128)S(1)}, s32[16]{0:T(128)}, u32[]{:S(2)}) copy-start(s32[16]{0:T(128)} %param.22) | copy-start | bytes 196
  12.4 8.2 %copy-start.7 = (s32[16]{0:T(128)S(1)}, s32[16]{0:T(128)}, u32[]{:S(2)}) copy-start(s32[16]{0:T(128)} %param.21) | copy-start | bytes 196
  12.4 11.9 %copy-start.5 = (bf16[1,256,2048]{2,1,0:T(8,128)(2,1)S(1)}, bf16[1,256,2048]{2,1,0:T(8,128)(2,1)}, u32[]{:S(2)}) copy-start(bf16[1,256,2048]{2,1,0:T(8,128)(2,1)} %param.19) | copy-start | bytes 3145732
  12.5 48.7 %all-to-all-start = ((bf16[16,32,2048]{2,1,0:T(8,128)(2,1)}), bf16[16,32,2048]{2,1,0:T(8,128)(2,1)}, u32[]{:S(2)}, u32[]{:S(2)}) async-start(bf16[16,32,2048]{2,1,0:T(8,128)(2,1)} %get-tuple-element.33), calls=%async_computation | async-start | bytes 4194304 | tf_op jit(solution)/shard_map/all_to_all | solution.py:367
  61.2 81.5 %all-to-all-start.1 = ((bf16[16,32,2048]{2,1,0:T(8,128)(2,1)}), bf16[16,32,2048]{2,1,0:T(8,128)(2,1)}, u32[]{:S(2)}, u32[]{:S(2)}) async-start(bf16[16,32,2048]{2,1,0:T(8,128)(2,1)} %get-tuple-element.35), calls=%async_computation.1 | async-start | bytes 4194304 | tf_op jit(solution)/shard_map/all_to_all | solution.py:367
  72.5 48.2 %collective-permute-start = (bf16[16,32,2048]{2,1,0:T(8,128)(2,1)}, bf16[16,32,2048]{2,1,0:T(8,128)(2,1)S(1)}, u32[]{:S(2)}, u32[]{:S(2)}) collective-permute-start(bf16[16,32,2048]{2,1,0:T(8,128)(2,1)} %all-to-all-done.refs_0_), channel_id=1, source_target_pairs={{0,1},{1,0},{2,3},{3,2},{4,5},{5,4},{6,7},{7,6},{8,9},{9,8},{10,11... | collective-permute-start | bytes 6291464 | tf_op jit(solution)/shard_map/ppermute | solution.py:409
  120.6 1.3 copy-start.9
  141.3 1.3 copy-start.4
  142.6 47.3 %collective-permute-start.1 = (bf16[16,32,2048]{2,1,0:T(8,128)(2,1)}, bf16[16,32,2048]{2,1,0:T(8,128)(2,1)S(1)}, u32[]{:S(2)}, u32[]{:S(2)}) collective-permute-start(bf16[16,32,2048]{2,1,0:T(8,128)(2,1)} %all-to-all-done.1.refs_0_), channel_id=1, source_target_pairs={{0,1},{1,0},{2,3},{3,2},{4,5},{5,4},{6,7},{7,6},{8,9},{9,8},{10,11... | collective-permute-start | bytes 6291464 | tf_op jit(solution)/shard_map/ppermute | solution.py:409
  189.9 1.3 copy-start.8
  199.7 1.3 copy-start.3
  258.8 6.0 %copy-start.2 = (s32[16]{0:T(128)S(1)}, s32[16]{0:T(128)}, u32[]{:S(2)}) copy-start(s32[16]{0:T(128)} %order_ref.1) | copy-start | bytes 196
  258.8 67.6 %all-to-all-start.2 = ((bf16[16,64,1024]{2,1,0:T(8,128)(2,1)}), bf16[16,64,1024]{2,1,0:T(8,128)(2,1)}, u32[]{:S(2)}, u32[]{:S(2)}) async-start(bf16[16,64,1024]{2,1,0:T(8,128)(2,1)} %get-tuple-element.46), calls=%async_computation.2 | async-start | bytes 4194304 | tf_op jit(solution)/shard_map/all_to_all | solution.py:367
  263.9 58.4 %all-gather.3.cloned.1.call-start = ((), (), s32[]{:S(2)}) async-start(), calls=%async_computation.9 | async-start | bytes 1114112 | tf_op jit(solution)/shard_map/all_gather | solution.py:444
  264.7 108.6 %reduce-scatter.3.cloned.1.call-start = ((), (), s32[]{:S(2)}) async-start(), calls=%async_computation.7 | async-start | bytes 3145728 | tf_op jit(solution)/shard_map/reduce_scatter | solution.py:463
  335.7 69.6 %reduce-scatter.5.cloned.1.call-start = ((), (), s32[]{:S(2)}) async-start(), calls=%async_computation.8 | async-start | bytes 3145728 | tf_op jit(solution)/shard_map/reduce_scatter | solution.py:463
Sparse Core Ops, SparseCore 0:
  266.9 55.3 all-gather.2
  335.8 30.4 reduce-scatter.2
  373.4 31.8 reduce-scatter.4

commit v3 on v2

v3 whole, which is shorter than its diff:
```python
import functools
import math

import jax
import jax.numpy as jnp
from jax import lax
from jax.experimental import pallas as pl
from jax.experimental.pallas import tpu as pltpu
from jax.sharding import PartitionSpec as P

HEAD_DIM = 128
KEY_BLOCK = 1024
ROW_BLOCK = 256
STATS = 128
VMEM_LIMIT = 50 * 1024 * 1024

rope_base = 10000.0
norm_eps = 1e-05
LOG2E = math.log2(math.e)
LOWEST = -1e30


def params():
    return pltpu.CompilerParams(vmem_limit_bytes=VMEM_LIMIT)


def layer_norm(token_rows):
    widened = token_rows.astype(jnp.float32)
    centred = widened - jnp.mean(widened, axis=-1, keepdims=True)
    variance = jnp.mean(centred * centred, axis=-1, keepdims=True)
    return centred * lax.rsqrt(variance + norm_eps)


def rope_tables(positions):
    half_dim = HEAD_DIM // 2
    frequency = jnp.exp(-jnp.log(rope_base) * jnp.arange(half_dim, dtype=jnp.float32) / half_dim)
    angles = positions.astype(jnp.float32)[:, None] * frequency[None, :]
    cosine = jnp.cos(angles)
    sine = jnp.sin(angles)
    return (
        jnp.concatenate([cosine, cosine], axis=-1),
        jnp.concatenate([-sine, sine], axis=-1),
    )


def deal_kernel(order_ref, tp_ref, x_ref, first_ref, second_ref, guest_ref):
    each, cut, _ = first_ref.shape
    start = pl.program_id(0) * each
    for at in range(each):
        normed = layer_norm(x_ref[order_ref[start + at]]).astype(jnp.bfloat16)
        first_ref[at] = normed[:cut]
        second_ref[at] = normed[cut:]
        guest_ref[at] = normed


def deal(tokens, deal_order, tp_index, piece):
    groups, _, width = tokens.shape
    each = 4
    steps = groups // each
    cut = piece // 2
    return pl.pallas_call(
        deal_kernel,
        grid_spec=pltpu.PrefetchScalarGridSpec(
            num_scalar_prefetch=2,
            grid=(steps,),
            in_specs=[pl.BlockSpec((groups, piece, width), lambda d, order, t: (0, t[0], 0))],
            out_specs=[
                pl.BlockSpec((each, cut, width), lambda d, order, t: (d, 0, 0)),
                pl.BlockSpec((each, cut, width), lambda d, order, t: (d, 0, 0)),
                pl.BlockSpec(
                    (each, piece, width), lambda d, order, t: ((d + steps // 2) % steps, 0, 0)
                ),
            ],
        ),
        out_shape=[
            jax.ShapeDtypeStruct((groups, rows, width), jnp.bfloat16) for rows in (cut, cut, piece)
        ],
        compiler_params=params(),
        name="deal",
    )(deal_order, tp_index, tokens)


def project_kernel(turned, heads, sources, tp_ref, *refs):
    if sources > 1:
        part_refs, (cos_ref, sin_ref, *refs, x_ref) = refs[:sources], refs[sources:]
        shards_in = part_refs[0].shape[0]
        half = x_ref.shape[0] // 2
        each = half // shards_in

        @pl.when(pl.program_id(0) == 0)
        def _():
            t = tp_ref[0]
            for shard in range(shards_in):
                at = shard * each
                for mine_ref, other_ref in zip(part_refs[::2], part_refs[1::2]):
                    piece = mine_ref.shape[1]
                    for part_ref, side in ((mine_ref, t), (other_ref, 1 - t)):
                        start = pl.multiple_of(side * half + at, piece)
                        x_ref[pl.ds(start, piece), :] = part_ref[shard]
                    at += piece
    else:
        x_ref, cos_ref, sin_ref, *refs = refs
    count = len(turned)
    step = min(256, x_ref.shape[0])
    for first in range(0, x_ref.shape[0], step):
        rows = slice(first, first + step)
        for w_ref, out_ref, turn in zip(refs[:count], refs[count:], turned):
            product = jnp.dot(x_ref[rows, :], w_ref[...], preferred_element_type=jnp.float32)
            if not turn:
                out_ref[rows, :] = product.astype(jnp.bfloat16)
                continue
            for head in range(heads):
                cut = slice(head * HEAD_DIM, (head + 1) * HEAD_DIM)
                part = product[:, cut]
                swapped = pltpu.roll(part, HEAD_DIM // 2, 1)
                out_ref[rows, cut] = (
                    part * cos_ref[rows, :] + swapped * sin_ref[rows, :]
                ).astype(jnp.bfloat16)


def project(x, tp_index, tables, weights, turned):
    depth = x[0].shape[-1]
    rows = sum(math.prod(part.shape[:-1]) for part in x)
    width = weights[0].shape[1]
    block = min(256, width)
    table = pl.BlockSpec((rows, HEAD_DIM), lambda n, t: (0, 0))
    count = len(weights)
    return pl.pallas_call(
        functools.partial(project_kernel, turned, block // HEAD_DIM, len(x)),
        grid_spec=pltpu.PrefetchScalarGridSpec(
            num_scalar_prefetch=1,
            grid=(width // block,),
            in_specs=[pl.BlockSpec(part.shape, lambda n, t, r=part.ndim: (0,) * r) for part in x]
            + [table, table]
            + [pl.BlockSpec((depth, block), lambda n, t: (0, n))] * count,
            out_specs=[pl.BlockSpec((rows, block), lambda n, t: (0, n))] * count,
            scratch_shapes=[pltpu.VMEM((rows, depth), jnp.bfloat16)] if len(x) > 1 else [],
        ),
        out_shape=[jax.ShapeDtypeStruct((rows, width), jnp.bfloat16)] * count,
        compiler_params=params(),
        cost_estimate=pl.CostEstimate(
            flops=2 * rows * depth * width * count,
            bytes_accessed=2 * (rows * depth + count * width * (rows + depth)),
            transcendentals=0,
        ),
        name="project",
    )(tp_index, *x, *tables, *weights)


def replace_kernel(block, index_ref, cache_ref, fresh_ref, out_ref):
    first = pl.program_id(1) * block
    count = index_ref.shape[1]
    row = first + lax.broadcasted_iota(jnp.int32, (block, count), 0)
    hits = jnp.where(row == index_ref[...], 1.0, 0.0)
    picked = jnp.dot(
        hits.astype(jnp.bfloat16), fresh_ref[0], preferred_element_type=jnp.float32
    )
    is_hit = jnp.sum(hits, axis=1, keepdims=True) > 0.5
    out_ref[0] = jnp.where(is_hit, picked, cache_ref[0, 0].astype(jnp.float32)).astype(jnp.bfloat16)


def replace_rows(cache, fresh, rec_index):
    _, _, rows, width = cache.shape
    count = rec_index.shape[1]
    block = 512
    return pl.pallas_call(
        functools.partial(replace_kernel, block),
        grid=(2, rows // block),
        in_specs=[
            pl.BlockSpec((1, count), lambda c, r: (0, 0)),
            pl.BlockSpec((1, 1, block, width), lambda c, r: (0, c, r, 0)),
            pl.BlockSpec((1, count, width), lambda c, r: (c, 0, 0)),
        ],
        out_specs=pl.BlockSpec((1, block, width), lambda c, r: (c, r, 0)),
        out_shape=jax.ShapeDtypeStruct((2, rows, width), jnp.bfloat16),
        compiler_params=params(),
        cost_estimate=pl.CostEstimate(
            flops=4 * rows * count * width, bytes_accessed=10 * rows * width, transcendentals=0
        ),
        name="replace_rows",
    )(rec_index, cache, fresh)


def fold_keys(jobs, m_ref, acc_ref):
    scale = HEAD_DIM**-0.5 * LOG2E

    def scores_of(job):
        _, queries, keys, _, mask = job
        scores = lax.dot_general(
            queries(), keys(), (((1,), (1,)), ((), ())), preferred_element_type=jnp.float32
        )
        return scores if mask is None else jnp.where(mask, scores, LOWEST)

    upcoming = scores_of(jobs[0])
    for at, (place, _, _, values, _) in enumerate(jobs):
        scores = upcoming
        if at + 1 < len(jobs):
            upcoming = scores_of(jobs[at + 1])
        old_max = m_ref[place]
        new_max = jnp.maximum(old_max, jnp.max(scores, axis=1, keepdims=True))
        factor = jnp.exp2((old_max - new_max) * scale)
        shift = new_max * scale
        tiles = scores.shape[1] // HEAD_DIM
        weights = jnp.exp2(scores * scale - jnp.concatenate([shift] * tiles, axis=1))
        seen = values()
        widened = jnp.concatenate([seen, jnp.ones(seen.shape, jnp.bfloat16)], axis=1)
        product = jnp.dot(
            weights.astype(jnp.bfloat16), widened, preferred_element_type=jnp.float32
        )
        acc_ref[place] = acc_ref[place] * jnp.concatenate([factor, factor], axis=1) + product
        m_ref[place] = new_max


def attend_kernel(causal, chunk, chunks, piece, count_ref, q_ref, k_ref, v_ref, *refs):
    if causal:
        nk_ref, nv_ref, *refs = refs
    o_ref, lse_ref, m_ref, acc_ref = refs
    scale = HEAD_DIM**-0.5 * LOG2E
    rows_in = q_ref.shape[0]
    per_step = q_ref.shape[1] // HEAD_DIM
    step = pl.program_id(0)
    used = count_ref[0]
    blocks = range(rows_in // ROW_BLOCK)
    places = [(head, block) for head in range(per_step) for block in blocks]
    m_ref[...] = jnp.full(m_ref.shape, LOWEST, jnp.float32)
    acc_ref[...] = jnp.zeros(acc_ref.shape, jnp.float32)
    k_all = k_ref.at[(0,) * (len(k_ref.shape) - 2)]
    v_all = v_ref.at[(0,) * (len(v_ref.shape) - 2)]

    def head_cut(head):
        return slice(head * HEAD_DIM, (head + 1) * HEAD_DIM)

    def rows_of(block):
        return slice(block * ROW_BLOCK, (block + 1) * ROW_BLOCK)

    def job(place, keys_ref, values_ref, picked, mask):
        head, block = place
        cut = head_cut(head)
        return (
            place,
            lambda: q_ref[rows_of(block), cut],
            lambda: keys_ref[picked, cut],
            lambda: values_ref[picked, cut],
            mask,
        )

    def visit(block, masked):
        start = pl.multiple_of(block * KEY_BLOCK, KEY_BLOCK)
        mask = None
        if masked:
            mask = lax.broadcasted_iota(jnp.int32, (1, KEY_BLOCK), 1) < used - start
        picked = pl.ds(start, KEY_BLOCK)
        fold_keys([job(place, k_all, v_all, picked, mask) for place in places], m_ref, acc_ref)

    full = used // KEY_BLOCK
    pl.loop(0, full)(lambda block: visit(block, False))

    @pl.when(used % KEY_BLOCK > 0)
    def _():
        visit(full, True)

    if causal:
        shards_each = ROW_BLOCK // piece
        jobs = []
        for place in places:
            row = lax.broadcasted_iota(jnp.int32, (ROW_BLOCK, ROW_BLOCK), 0)
            key = lax.broadcasted_iota(jnp.int32, (ROW_BLOCK, ROW_BLOCK), 1)
            row_shard, key_shard = row // piece, key // piece
            for key_chunk in range(chunks):
                same = key % piece <= row % piece if key_chunk == chunk else key_chunk < chunk
                mask = (key_shard < row_shard) | ((key_shard == row_shard) & same)
                first = key_chunk * rows_in
                for key_block in range(place[1] + 1):
                    at = first + key_block * ROW_BLOCK
                    picked = slice(at, at + ROW_BLOCK)
                    is_last = key_block == place[1]
                    jobs.append(job(place, nk_ref, nv_ref, picked, mask if is_last else None))
        fold_keys(jobs, m_ref, acc_ref)

    for head, block in places:
        rows = rows_of(block)
        total = acc_ref[head, block, :, HEAD_DIM:]
        seen = total > 0.0
        safe = jnp.where(seen, total, 1.0)
        out = (acc_ref[head, block, :, :HEAD_DIM] / safe).astype(jnp.bfloat16)
        column = step * per_step + head
        o_ref[rows, pl.ds(pl.multiple_of(column * HEAD_DIM, HEAD_DIM), HEAD_DIM)] = out
        lse = jnp.where(seen, m_ref[head, block] * scale + jnp.log2(safe), LOWEST)
        lane = lax.broadcasted_iota(jnp.int32, (ROW_BLOCK, STATS), 1)
        before = jnp.where(column == 0, 0.0, lse_ref[rows, :])
        lse_ref[rows, :] = jnp.where(lane == column, lse, before)

    @pl.when(step == pl.num_programs(0) - 1)
    def _():
        for block in blocks:
            rows = rows_of(block)
            left = lse_ref[rows, :]
            packed = jnp.zeros_like(left)
            for turn in range(3):
                part = left.astype(jnp.bfloat16).astype(jnp.float32)
                left = left - part
                packed = packed + (pltpu.roll(part, turn * STATS // 4, 1) if turn else part)
            o_ref[rows, o_ref.shape[1] - STATS :] = packed.astype(jnp.bfloat16)


def attend(count, groups, chunk, chunks, queries, cache, new_keys=None, new_values=None):
    span, width = queries.shape
    heads = width // HEAD_DIM
    per_step = 2
    rows = cache.shape[-2]
    causal = new_keys is not None
    rows_in = span // chunks
    lead = cache.ndim - 3
    shape = (1,) * (lead + 1) + (rows, per_step * HEAD_DIM)
    every = pl.BlockSpec((span, per_step * HEAD_DIM), lambda h, n: (0, h))

    def half(which):
        return pl.BlockSpec(shape, lambda h, n: (0,) * lead + (which, 0, h))

    keys_seen = rows + (span // 2 if causal else 0)
    out = pl.pallas_call(
        functools.partial(attend_kernel, causal, chunk, chunks, rows_in // groups),
        grid_spec=pltpu.PrefetchScalarGridSpec(
            num_scalar_prefetch=1,
            grid=(heads // per_step,),
            in_specs=[
                pl.BlockSpec((rows_in, per_step * HEAD_DIM), lambda h, n: (chunk, h)),
                half(0),
                half(1),
            ]
            + [every] * (2 if causal else 0),
            out_specs=pl.BlockSpec((rows_in, width + STATS), lambda h, n: (0, 0)),
            scratch_shapes=[
                pltpu.VMEM((rows_in, STATS), jnp.float32),
                pltpu.VMEM((per_step, rows_in // ROW_BLOCK, ROW_BLOCK, HEAD_DIM), jnp.float32),
                pltpu.VMEM((per_step, rows_in // ROW_BLOCK, ROW_BLOCK, 2 * HEAD_DIM), jnp.float32),
            ],
        ),
        out_shape=jax.ShapeDtypeStruct((rows_in, width + STATS), jnp.bfloat16),
        compiler_params=params(),
        cost_estimate=pl.CostEstimate(
            flops=16 * rows_in * keys_seen * width,
            bytes_accessed=4 * rows * width + 4 * rows_in * width,
            transcendentals=rows_in * keys_seen * heads,
        ),
        name="attend_own" if causal else "attend_guest",
    )(count, queries, cache, cache, *((new_keys, new_values) if causal else ()))
    return out.reshape(groups, rows_in // groups, width + STATS)


def merge_kernel(groups, heads, inverse_ref, tp_ref, own_ref, guest_ref, w_ref, *refs):
    *out_refs, att_ref = refs
    piece = own_ref.shape[1]
    width = heads * HEAD_DIM
    step = pl.program_id(0)

    def stats(part_ref, at):
        packed = part_ref[at, :, width:].astype(jnp.float32)
        return (
            packed
            + pltpu.roll(packed, STATS - STATS // 4, 1)
            + pltpu.roll(packed, STATS - STATS // 2, 1)
        )

    @pl.when(step == 0)
    def _():
        def one_request(request, carry):
            source = inverse_ref[request]
            helper = lax.rem(source + groups // 2, groups)
            own_lse = stats(own_ref, source)
            guest_lse = stats(guest_ref, helper)
            top = jnp.maximum(own_lse, guest_lse)
            own_share = jnp.exp2(own_lse - top)
            guest_share = jnp.exp2(guest_lse - top)
            total = own_share + guest_share
            own_share = own_share / total
            guest_share = guest_share / total
            rows = pl.ds(pl.multiple_of(request * piece, piece), piece)
            for head in range(heads):
                cut = slice(head * HEAD_DIM, (head + 1) * HEAD_DIM)
                merged = own_ref[source, :, cut].astype(jnp.float32) * own_share[
                    :, head : head + 1
                ] + guest_ref[helper, :, cut].astype(jnp.float32) * guest_share[:, head : head + 1]
                att_ref[rows, cut] = merged.astype(jnp.bfloat16)
            return carry

        lax.fori_loop(0, groups, one_request, 0)

    product = jnp.dot(att_ref[...], w_ref[...], preferred_element_type=jnp.float32).astype(
        jnp.bfloat16
    )
    each = pl.num_programs(0) // len(out_refs)
    for at, out_ref in enumerate(out_refs):
        pl.when(step // each == at)(functools.partial(out_ref.__setitem__, ..., product))


def merge(inverse, tp_index, splits, own, guest, w_out):
    groups, piece, padded = guest.shape
    width = w_out.shape[0]
    heads = width // HEAD_DIM
    columns = w_out.shape[1]
    block = 512
    rows = groups * piece
    steps = columns // block
    each = steps // splits

    def w_at(n, i, t):
        return (0, (n + each * (1 - t[0])) % steps if splits == 2 else n)

    def out_at(which):
        return lambda n, i, t: (0, jnp.clip(n - which * each, 0, each - 1))

    part = pl.BlockSpec(guest.shape, lambda n, i, t: (0, 0, 0))
    return pl.pallas_call(
        functools.partial(merge_kernel, groups, heads),
        grid_spec=pltpu.PrefetchScalarGridSpec(
            num_scalar_prefetch=2,
            grid=(steps,),
            in_specs=[part, part, pl.BlockSpec((width, block), w_at)],
            out_specs=[pl.BlockSpec((rows, block), out_at(which)) for which in range(splits)],
            scratch_shapes=[pltpu.VMEM((rows, width), jnp.bfloat16)],
        ),
        out_shape=[jax.ShapeDtypeStruct((rows, columns // splits), jnp.bfloat16)] * splits,
        compiler_params=params(),
        cost_estimate=pl.CostEstimate(
            flops=4 * rows * width * columns,
            bytes_accessed=2 * (2 * rows * padded + width * columns + rows * columns),
            transcendentals=0,
        ),
        name="merge",
    )(inverse, tp_index, own, guest, w_out)


def exchange(value):
    return lax.all_to_all(value, "grp", split_axis=0, concat_axis=0, tiled=True)


def shards(
    tokens,
    w_query,
    w_key,
    w_value,
    w_out,
    own_cache,
    guest_cache,
    rec_hidden,
    deal_order,
    own_len,
    guest_len,
    rec_index,
):
    groups = lax.axis_size("grp")
    tp_size = lax.axis_size("tp")
    group_id = lax.axis_index("grp")
    tp_id = lax.axis_index("tp")
    partner_id = (group_id + groups // 2) % groups
    width = w_query.shape[1]
    heads = width // HEAD_DIM
    shard_rows = tokens.shape[1]
    span = shard_rows * groups
    piece = shard_rows // tp_size

    chunks = 2
    chunk_rows = shard_rows // chunks
    paired = tp_size == 2 and piece % 32 == 0
    tp_index = tp_id.astype(jnp.int32)[None]
    tied = lax.optimization_barrier
    neighbour = [(0, 1), (1, 0)]

    if paired:
        *own_rows, guest_rows = deal(tokens, deal_order, tp_index, piece)
    else:
        mine = lax.dynamic_slice_in_dim(tokens, tp_id * piece, piece, 1)
        normed = layer_norm(mine).astype(jnp.bfloat16)
        own_rows = [jnp.take(normed, deal_order, axis=0)]
        guest_rows = jnp.roll(own_rows[0], groups // 2, axis=0)

    def gathered(arrived):
        if paired:
            return [arrived, lax.ppermute(arrived, "tp", neighbour)]
        arrived = lax.all_gather(arrived, "tp", axis=0)
        arrived = jnp.transpose(arrived, (1, 0, 2, 3)).reshape(groups, chunks, chunk_rows, -1)
        return [jnp.transpose(arrived, (1, 0, 2, 3)).reshape(span, -1)]

    def place(owner, helper):
        row = jnp.arange(span, dtype=jnp.int32).reshape(groups, chunks, chunk_rows)
        row = jnp.transpose(row, (1, 0, 2)).reshape(span)
        return own_len[owner] + guest_len[helper] + row

    own_x = gathered(exchange(own_rows[0]))
    if paired:
        own_x[0], own_rows[1] = tied((own_x[0], own_rows[1]))
        second = exchange(own_rows[1])
    own_tables = rope_tables(place(group_id, partner_id))
    guest_tables = rope_tables(place(partner_id, group_id))
    rec_tables = rope_tables(rec_index[0])
    rec_rows = layer_norm(rec_hidden[0]).astype(jnp.bfloat16)
    rec_keys, rec_values = project((rec_rows,), tp_index, rec_tables, (w_key, w_value), (True, False))
    cache = replace_rows(own_cache, jnp.stack([rec_keys, rec_values]), rec_index)
    if paired:
        second, cache, own_tables, guest_tables, own_x, guest_rows = tied(
            (second, cache, own_tables, guest_tables, own_x, guest_rows)
        )
        own_x = own_x + gathered(second)

    guest_arrived = exchange(guest_rows)
    queries, new_keys, new_values = project(
        own_x, tp_index, own_tables, (w_query, w_key, w_value), (True, True, False)
    )
    guest_arrived, queries = tied((guest_arrived, queries))
    guest_x = gathered(guest_arrived)

    def own_attend(chunk, seen):
        return attend(own_len[group_id][None], groups, chunk, chunks, seen, cache, new_keys, new_values)

    def guest_attend(chunk, seen):
        return attend(guest_len[group_id][None], groups, chunk, chunks, seen, guest_cache)

    own_out = [own_attend(0, queries)]
    own_out[0], queries = tied((own_out[0], queries))
    own_out.append(own_attend(1, queries))
    own_part = [exchange(own_out[0])]
    guest_x, own_out[1] = tied((guest_x, own_out[1]))
    (guest_queries,) = project(guest_x, tp_index, guest_tables, (w_query,), (True,))
    own_part[0], guest_queries, own_out[1] = tied((own_part[0], guest_queries, own_out[1]))
    own_part.append(exchange(own_out[1]))
    guest_out = [guest_attend(0, guest_queries)]
    guest_out[0], guest_queries = tied((guest_out[0], guest_queries))
    guest_out.append(guest_attend(1, guest_queries))
    own_part[1], guest_out = tied((own_part[1], guest_out))

    inverse = jnp.sum(
        jnp.where(
            deal_order[None, :] == jnp.arange(groups, dtype=deal_order.dtype)[:, None],
            jnp.arange(groups, dtype=jnp.int32)[None, :],
            0,
        ),
        axis=1,
    )
    guest_part = [exchange(guest_out[0])]
    guest_part[0], guest_out[1] = tied((guest_part[0], guest_out[1]))
    guest_part.append(exchange(guest_out[1]))
    mixed = []
    for chunk in range(chunks):
        partial = merge(
            inverse, tp_index, 2 if paired else 1, own_part[chunk], guest_part[chunk], w_out
        )
        if chunk == 0:
            partial, guest_part[1] = tied((partial, guest_part[1]))
        if paired:
            theirs, mine = partial
            arrived = lax.ppermute(theirs, "tp", neighbour).astype(jnp.float32)
            summed = (mine.astype(jnp.float32) + arrived).astype(jnp.bfloat16)
        else:
            summed = lax.psum_scatter(partial[0], "tp", scatter_dimension=1, tiled=True)
        mixed.append(summed.reshape(groups, chunk_rows, -1))
    return jnp.concatenate(mixed, axis=1)


def solution(mesh):
    return jax.shard_map(
        shards,
        mesh=mesh,
        in_specs=(
            P(None, "grp", None),
            P(None, "tp"),
            P(None, "tp"),
            P(None, "tp"),
            P("tp", None),
            P("grp", None, None, "tp"),
            P("grp", None, None, "tp"),
            P("grp", None, None),
            P(),
            P(),
            P(),
            P("grp", None),
        ),
        out_specs=P(None, "grp", "tp"),
        check_vma=False,
    )
```

time: 416 us -> 347 us (0.83)
  waiting for transfers between devices: 158 us -> 95.1 us
  blocking collectives: 56.9 us -> 33.7 us
  starting transfers between devices: 27.2 us -> 43.5 us
  between operations: 15.7 us -> 2.65 us
  Pallas kernels: 136 us -> 148 us
    all_gather x1 -> x0, waiting for transfers between devices: 57.5 us -> none  [shards(): lax.all_gather(jnp.concatenate([own_lse, guest_lse])[:, 0], 'grp', axis=0)]
    reduce_scatter x2 -> x0, waiting for transfers between devices: 32 us -> none  [shards(): summed = lax.psum_scatter(partial, 'tp', scatter_dimension=1, tiled=True)]
    all_to_all x2 -> x1, blocking collectives: 56.9 us -> 33.7 us  [exchange(): return lax.all_to_all(value, 'grp', split_axis=0, concat_axis=0, tiled=True)]
    all_to_all x3 -> x6, waiting for transfers between devices: 14.9 us -> 32 us  [exchange(): return lax.all_to_all(value, 'grp', split_axis=0, concat_axis=0, tiled=True)]
    all_to_all x3 -> x6, starting transfers between devices: 24 us -> 36.6 us  [exchange(): return lax.all_to_all(value, 'grp', split_axis=0, concat_axis=0, tiled=True)]
    pallas_call x2 -> x4, Pallas kernels: 67.8 us -> 79.7 us  [attend(): pl.pallas_call(functools.partial(attend_kernel, causal, chunk, chunks, ro...]
    ppermute x2 -> x5, waiting for transfers between devices: 53.5 us -> 63.2 us  [the longest x2 36.1 us: shards(): arrived = lax.ppermute(theirs, 'tp', neighbour).astype(jnp.float32)]
    unnamed x22 -> x28, local copies, waits for them, and re-layouts: 8.37 us -> 10.9 us
  transfers between devices with their start and end apart: 8 -> 11, of which waited for: 5 -> 6; matrix products, arithmetic and copies ran while one was open for 3% -> 2% of each run, Pallas kernels for 20% -> 42%
where the time goes in v3:
time: 347 us; the launch traced here: 344 us
  Pallas kernels  148 us (43%)
  waiting for transfers between devices  95.1 us (27%)
  starting transfers between devices  43.5 us (13%)
  blocking collectives  33.7 us (10%)
  local copies, waits for them, and re-layouts  12.3 us (4%)
  other arithmetic  8.61 us (2%)
    pallas_call x4, Pallas kernels, attend(): pl.pallas_call(functools.partial(attend_kernel, causal, chunk, chunks, ro...  79.7 us
    all_to_all x6, starting transfers between devices, exchange(): return lax.all_to_all(value, 'grp', split_axis=0, concat_axis=0, tiled=True)  36.6 us
    ppermute x2, waiting for transfers between devices, shards(): arrived = lax.ppermute(theirs, 'tp', neighbour).astype(jnp.float32)  36.1 us
    all_to_all x1, blocking collectives, exchange(): return lax.all_to_all(value, 'grp', split_axis=0, concat_axis=0, tiled=True)  33.7 us
    pallas_call x3, Pallas kernels, project(): pl.pallas_call(functools.partial(project_kernel, turned, block // HEAD_DI...  33 us
    all_to_all x6, waiting for transfers between devices, exchange(): return lax.all_to_all(value, 'grp', split_axis=0, concat_axis=0, tiled=True)  32 us
    ppermute x3, waiting for transfers between devices, gathered(): return [arrived, lax.ppermute(arrived, 'tp', neighbour)]  27.1 us
    pallas_call x2, Pallas kernels, merge(): pl.pallas_call(functools.partial(merge_kernel, groups, heads), grid_spec=...  19.9 us
  transfers between devices with their start and end apart: 11, of which 6 were waited for; matrix products, arithmetic and copies ran while one was open for 2% of the time, Pallas kernels for 42%

profile of v3, /device:TPU:0, one launch (start us, length us, event | category | flops | bytes accessed | tf_op | source)
XLA Modules:
  0.0 344.1 jit_solution(7619300378394962264)
XLA Ops:
  0.7 5.1 %deal.1 = (bf16[16,16,2048]{2,1,0:T(8,128)(2,1)}, bf16[16,16,2048]{2,1,0:T(8,128)(2,1)}, bf16[16,32,2048]{2,1,0:T(8,128)(2,1)}) custom-call(s32[16]{0:T(128)S(1)} %copy-done.1, s32[1]{0:T(128)} %bitcast.tp_ref, bf16[16,64,2048]{2,1,0:T(8,128)(2,1)} %x_ref.1), custom_call_target="tpu_custom_call" | custom-call | tf_op jit(solution)/shard_map/deal/pallas_call | solution.py:61
  5.8 7.5 %all-to-all-start = ((bf16[16,16,2048]{2,1,0:T(8,128)(2,1)}), bf16[16,16,2048]{2,1,0:T(8,128)(2,1)S(1)}, u32[]{:S(2)}, u32[]{:S(2)}) async-start(bf16[16,16,2048]{2,1,0:T(8,128)(2,1)} %get-tuple-element.48), calls=%async_computation | async-start | bytes 2097152 | tf_op jit(solution)/shard_map/all_to_all | solution.py:435
  18.4 17.9 %all-to-all-done.refs_0_ = bf16[16,16,2048]{2,1,0:T(8,128)(2,1)S(1)} async-done(((bf16[16,16,2048]{2,1,0:T(8,128)(2,1)}), bf16[16,16,2048]{2,1,0:T(8,128)(2,1)S(1)}, u32[]{:S(2)}, u32[]{:S(2)}) %all-to-all-start) | async-done | bytes 1048608 | tf_op jit(solution)/shard_map/all_to_all | solution.py:435
  36.3 6.9 %all-to-all-start.1 = ((bf16[16,16,2048]{2,1,0:T(8,128)(2,1)}), bf16[16,16,2048]{2,1,0:T(8,128)(2,1)}, u32[]{:S(2)}, u32[]{:S(2)}) async-start(bf16[16,16,2048]{2,1,0:T(8,128)(2,1)} %get-tuple-element.50), calls=%async_computation.1 | async-start | bytes 2097152 | tf_op jit(solution)/shard_map/all_to_all | solution.py:435
  43.7 1.6 collective-permute-start
  45.3 5.8 %project.3 = (bf16[256,1024]{1,0:T(8,128)(2,1)S(1)}, bf16[256,1024]{1,0:T(8,128)(2,1)S(1)}) custom-call(s32[1]{0:T(128)} %bitcast.tp_ref, bf16[256,2048]{1,0:T(8,128)(2,1)S(1)} %fusion.4.refs_0_, f32[256,128]{1,0:T(8,128)S(1)} %get-tuple-element.107.refs_1_, f32[256,128]{1,0:T(8,128)S(1)} %get-tuple-element.108.refs_2_, bf16[2048,1024]{1,0:T(8,128)(2,1)} %refs_7_.1, ...), custom_call_target="tpu_custom_call" | custom-call | flops 2147483648 | bytes 10485760 | tf_op jit(solution)/shard_map/project/pallas_call | solution.py:128
  51.2 3.7 %fusion.6 = (f32[1024,64]{1,0:T(8,128)S(1)}, f32[1024,64]{1,0:T(8,128)S(1)}, f32[1024,64]{1,0:T(8,128)S(1)}, f32[1024,64]{1,0:T(8,128)S(1)}, f32[1024,64]{1,0:T(8,128)S(1)}, /*index=5*/f32[1024,64]{1,0:T(8,128)S(1)}) fusion(f32[64]{0:T(128)S(1)} %multiply_exponential_fusion, f32[1024]{0:T(1024)S(1)} %reshape.124, f32[1024]{0:T(1024)S(1)} %reshape.123), kind=kLoop, calls=%fused_computation.22 | loop fusion | flops 262144 | bytes 1581312 | tf_op jit(solution)/shard_map/neg | solution.py:42
  55.6 10.6 %replace_rows.1.k_ref.v_ref = bf16[2,2048,1024]{2,1,0:T(8,128)(2,1)} custom-call(s32[1,256]{1,0:T(1,128)S(1)} %copy-done, bf16[1,2,2048,1024]{3,2,1,0:T(8,128)(2,1)} %cache_ref.1, bf16[2,256,1024]{2,1,0:T(8,128)(2,1)S(1)} %pad_maximum_fusion.1.fresh_ref), custom_call_target="tpu_custom_call" | custom-call | flops 2147483648 | bytes 20971520 | tf_op jit(solution)/shard_map/replace_rows/pallas_call | solution.py:166
  66.2 3.0 collective-permute-done.refs_1_
  70.2 5.8 %all-to-all-start.2 = ((bf16[16,32,2048]{2,1,0:T(8,128)(2,1)}), bf16[16,32,2048]{2,1,0:T(8,128)(2,1)}, u32[]{:S(2)}, u32[]{:S(2)}) async-start(bf16[16,32,2048]{2,1,0:T(8,128)(2,1)} %get-tuple-element.55), calls=%async_computation.2 | async-start | bytes 4194304 | tf_op jit(solution)/shard_map/all_to_all | solution.py:435
  76.0 1.6 collective-permute-start.1
  77.6 24.1 %collective-permute-done.1.refs_3_ = bf16[16,16,2048]{2,1,0:T(8,128)(2,1)S(1)} collective-permute-done((bf16[16,16,2048]{2,1,0:T(8,128)(2,1)}, bf16[16,16,2048]{2,1,0:T(8,128)(2,1)S(1)}, u32[]{:S(2)}, u32[]{:S(2)}) %collective-permute-start.1) | collective-permute-done | bytes 1048608 | tf_op jit(solution)/shard_map/ppermute | solution.py:480
  103.9 18.4 %project.4 = (bf16[1024,1024]{1,0:T(8,128)(2,1)}, bf16[1024,1024]{1,0:T(8,128)(2,1)}, bf16[1024,1024]{1,0:T(8,128)(2,1)}) custom-call(s32[1]{0:T(128)} %bitcast.tp_ref, bf16[16,16,2048]{2,1,0:T(8,128)(2,1)S(1)} %all-to-all-done.refs_0_, bf16[16,16,2048]{2,1,0:T(8,128)(2,1)S(1)} %copy-done.4, bf16[16,16,2048]{2,1,0:T(8,128)(2,1)} %all-to-all-done.1.refs_2_, ...), custom_call_target="tpu_custom_call" | custom-call | flops 12884901888 | bytes 23068672 | tf_op jit(solution)/shard_map/project/pallas_call | solution.py:128
  122.3 1.6 collective-permute-start.2
  123.9 1.6 copy-done.8
  125.5 23.5 %attend_own.2 = bf16[512,1152]{1,0:T(8,128)(2,1)} custom-call(s32[1]{0:T(128)} %get-tuple-element.106.count_ref, bf16[1024,1024]{1,0:T(8,128)(2,1)S(1)} %copy-done.8, bf16[2,2048,1024]{2,1,0:T(8,128)(2,1)} %replace_rows.1.k_ref.v_ref, bf16[2,2048,1024]{2,1,0:T(8,128)(2,1)} %replace_rows.1.k_ref.v_ref, bf16[1024,1024]{1,0:T(8,128)(2,1)} %get-tuple-element.64.refs_0_, ...), custom_call_target="tpu_custom_call" | custom-call | flops 21474836480 | bytes 10485760 | tf_op jit(solution)/shard_map/attend_own/pallas_call | solution.py:321
  149.0 6.0 %all-to-all-start.3 = ((bf16[16,32,1152]{2,1,0:T(8,128)(2,1)}), bf16[16,32,1152]{2,1,0:T(8,128)(2,1)S(1)}, u32[]{:S(2)}, u32[]{:S(2)}) async-start(bf16[16,32,1152]{2,1,0:T(8,128)(2,1)} %bitcast.7), calls=%async_computation.3 | async-start | bytes 2359296 | tf_op jit(solution)/shard_map/all_to_all | solution.py:435
  155.0 1.6 copy-done.9
  156.5 23.4 %attend_own.3 = bf16[512,1152]{1,0:T(8,128)(2,1)} custom-call(s32[1]{0:T(128)} %get-tuple-element.106.count_ref, bf16[1024,1024]{1,0:T(8,128)(2,1)S(1)} %copy-done.9, bf16[2,2048,1024]{2,1,0:T(8,128)(2,1)} %replace_rows.1.k_ref.v_ref, bf16[2,2048,1024]{2,1,0:T(8,128)(2,1)} %replace_rows.1.k_ref.v_ref, bf16[1024,1024]{1,0:T(8,128)(2,1)} %get-tuple-element.64.refs_0_, ...), custom_call_target="tpu_custom_call" | custom-call | flops 21474836480 | bytes 10485760 | tf_op jit(solution)/shard_map/attend_own/pallas_call | solution.py:321
  180.0 8.8 %project.5.q_ref = bf16[1024,1024]{1,0:T(8,128)(2,1)S(1)} custom-call(s32[1]{0:T(128)} %bitcast.tp_ref, bf16[16,32,2048]{2,1,0:T(8,128)(2,1)} %all-to-all-done.2.refs_0_, bf16[16,32,2048]{2,1,0:T(8,128)(2,1)} %collective-permute-done.2.refs_1_, f32[1024,128]{1,0:T(8,128)S(1)} %get-tuple-element.71.refs_2_, f32[1024,128]{1,0:T(8,128)S(1)} %get-tuple-element.72.refs_3_, ...), custom_call_target="tpu_custom_call" | custom-call | flops 4294967296 | bytes 10485760 | tf_op jit(solution)/shard_map/project/pallas_call | solution.py:128
  190.1 6.0 %all-to-all-start.4 = ((bf16[16,32,1152]{2,1,0:T(8,128)(2,1)}), bf16[16,32,1152]{2,1,0:T(8,128)(2,1)S(1)}, u32[]{:S(2)}, u32[]{:S(2)}) async-start(bf16[16,32,1152]{2,1,0:T(8,128)(2,1)} %bitcast.8), calls=%async_computation.4 | async-start | bytes 2359296 | tf_op jit(solution)/shard_map/all_to_all | solution.py:435
  196.1 1.6 copy-done.7
  197.7 15.9 %attend_guest.2 = bf16[512,1152]{1,0:T(8,128)(2,1)S(1)} custom-call(s32[1]{0:T(128)} %get-tuple-element.103.count_ref, bf16[1024,1024]{1,0:T(8,128)(2,1)S(1)} %copy-done.7, bf16[1,2,2048,1024]{3,2,1,0:T(8,128)(2,1)} %v_ref.3, bf16[1,2,2048,1024]{3,2,1,0:T(8,128)(2,1)} %v_ref.3), custom_call_target="tpu_custom_call" | custom-call | flops 17179869184 | bytes 10485760 | tf_op jit(solution)/shard_map/attend_guest/pallas_call | solution.py:321
  213.6 16.9 %attend_guest.3 = bf16[512,1152]{1,0:T(8,128)(2,1)} custom-call(s32[1]{0:T(128)} %get-tuple-element.103.count_ref, bf16[1024,1024]{1,0:T(8,128)(2,1)S(1)} %copy-done.7, bf16[1,2,2048,1024]{3,2,1,0:T(8,128)(2,1)} %v_ref.3, bf16[1,2,2048,1024]{3,2,1,0:T(8,128)(2,1)} %v_ref.3), custom_call_target="tpu_custom_call" | custom-call | flops 17179869184 | bytes 10485760 | tf_op jit(solution)/shard_map/attend_guest/pallas_call | solution.py:321
  230.4 33.7 %all_to_all.35.guest_ref = bf16[16,32,1152]{2,1,0:T(8,128)(2,1)} all-to-all(bf16[16,32,1152]{2,1,0:T(8,128)(2,1)S(1)} %bitcast.24), channel_id=1, replica_groups=mesh['grp'=16,'tp'=2] {'grp'}, dimensions={0} | all-to-all | bytes 2359296 | tf_op jit(solution)/shard_map/all_to_all | solution.py:435
  264.1 4.4 %all-to-all-start.6 = ((bf16[16,32,1152]{2,1,0:T(8,128)(2,1)}), bf16[16,32,1152]{2,1,0:T(8,128)(2,1)}, u32[]{:S(2)}, u32[]{:S(2)}) async-start(bf16[16,32,1152]{2,1,0:T(8,128)(2,1)} %bitcast.10), calls=%async_computation.6 | async-start | bytes 2359296 | tf_op jit(solution)/shard_map/all_to_all | solution.py:435
  268.7 9.9 %merge.2 = (bf16[512,1024]{1,0:T(8,128)(2,1)S(1)}, bf16[512,1024]{1,0:T(8,128)(2,1)S(1)}) custom-call(s32[16]{0:T(128)S(1)} %select_reduce_fusion.inverse_ref, s32[1]{0:T(128)} %bitcast.tp_ref, bf16[16,32,1152]{2,1,0:T(8,128)(2,1)S(1)} %all-to-all-done.3.own_ref, bf16[16,32,1152]{2,1,0:T(8,128)(2,1)} %all_to_all.35.guest_ref, bf16[1024,2048]{1,0:T(8,128)(2,1)} %w_ref.3), custom_call_target="tpu_custom_call" | custom-call | flops 4294967296 | bytes 8650752 | tf_op jit(solution)/shard_map/merge/pallas_call | solution.py:414
  279.6 14.1 %all-to-all-done.6.guest_ref = bf16[16,32,1152]{2,1,0:T(8,128)(2,1)} async-done(((bf16[16,32,1152]{2,1,0:T(8,128)(2,1)}), bf16[16,32,1152]{2,1,0:T(8,128)(2,1)}, u32[]{:S(2)}, u32[]{:S(2)}) %all-to-all-start.6) | async-done | bytes 1179680 | tf_op jit(solution)/shard_map/all_to_all | solution.py:435
  294.2 9.9 %merge.3 = (bf16[512,1024]{1,0:T(8,128)(2,1)S(1)}, bf16[512,1024]{1,0:T(8,128)(2,1)S(1)}) custom-call(s32[16]{0:T(128)S(1)} %select_reduce_fusion.inverse_ref, s32[1]{0:T(128)} %bitcast.tp_ref, bf16[16,32,1152]{2,1,0:T(8,128)(2,1)S(1)} %all-to-all-done.4.own_ref, bf16[16,32,1152]{2,1,0:T(8,128)(2,1)} %all-to-all-done.6.guest_ref, bf16[1024,2048]{1,0:T(8,128)(2,1)} %w_ref.3), custom_call_target="tpu_custom_call" | custom-call | flops 4294967296 | bytes 8650752 | tf_op jit(solution)/shard_map/merge/pallas_call | solution.py:414
  304.1 1.6 collective-permute-start.4
  305.7 14.2 %collective-permute-done.3 = bf16[512,1024]{1,0:T(8,128)(2,1)S(1)} collective-permute-done((bf16[512,1024]{1,0:T(8,128)(2,1)}, bf16[512,1024]{1,0:T(8,128)(2,1)S(1)}, u32[]{:S(2)}, u32[]{:S(2)}) %collective-permute-start.3) | collective-permute-done | bytes 1048608 | tf_op jit(solution)/shard_map/ppermute | solution.py:552
  320.3 21.9 %collective-permute-done.4 = bf16[512,1024]{1,0:T(8,128)(2,1)S(1)} collective-permute-done((bf16[512,1024]{1,0:T(8,128)(2,1)S(1)}, bf16[512,1024]{1,0:T(8,128)(2,1)S(1)}, u32[]{:S(2)}, u32[]{:S(2)}) %collective-permute-start.4) | collective-permute-done | bytes 1048608 | tf_op jit(solution)/shard_map/ppermute | solution.py:552
  (53 shorter events, 12.9 us)
Async XLA Ops:
  0.0 0.7 copy-start.1
  5.8 7.5 %copy-start.11 = (s32[16]{0:T(128)S(1)}, s32[16]{0:T(128)}, u32[]{:S(2)}) copy-start(s32[16]{0:T(128)} %param.22) | copy-start | bytes 196
  5.8 8.1 %copy-start.12 = (s32[16]{0:T(128)S(1)}, s32[16]{0:T(128)}, u32[]{:S(2)}) copy-start(s32[16]{0:T(128)} %param.21) | copy-start | bytes 196
  5.8 11.3 %copy-start = (s32[1,256]{1,0:T(1,128)S(1)}, s32[1,256]{1,0:T(1,128)}, u32[]{:S(2)}) copy-start(s32[1,256]{1,0:T(1,128)} %index_ref.1) | copy-start | bytes 3076
  5.8 11.3 %copy-start.10 = (bf16[1,256,2048]{2,1,0:T(8,128)(2,1)S(1)}, bf16[1,256,2048]{2,1,0:T(8,128)(2,1)}, u32[]{:S(2)}) copy-start(bf16[1,256,2048]{2,1,0:T(8,128)(2,1)} %param.19) | copy-start | bytes 3145732
  5.8 30.5 %all-to-all-start = ((bf16[16,16,2048]{2,1,0:T(8,128)(2,1)}), bf16[16,16,2048]{2,1,0:T(8,128)(2,1)S(1)}, u32[]{:S(2)}, u32[]{:S(2)}) async-start(bf16[16,16,2048]{2,1,0:T(8,128)(2,1)} %get-tuple-element.48), calls=%async_computation | async-start | bytes 2097152 | tf_op jit(solution)/shard_map/all_to_all | solution.py:435
  36.3 33.9 %all-to-all-start.1 = ((bf16[16,16,2048]{2,1,0:T(8,128)(2,1)}), bf16[16,16,2048]{2,1,0:T(8,128)(2,1)}, u32[]{:S(2)}, u32[]{:S(2)}) async-start(bf16[16,16,2048]{2,1,0:T(8,128)(2,1)} %get-tuple-element.50), calls=%async_computation.1 | async-start | bytes 2097152 | tf_op jit(solution)/shard_map/all_to_all | solution.py:435
  43.7 25.5 %collective-permute-start = (bf16[16,16,2048]{2,1,0:T(8,128)(2,1)S(1)}, bf16[16,16,2048]{2,1,0:T(8,128)(2,1)S(1)}, u32[]{:S(2)}, u32[]{:S(2)}) collective-permute-start(bf16[16,16,2048]{2,1,0:T(8,128)(2,1)S(1)} %all-to-all-done.refs_0_), channel_id=1, source_target_pairs={{0,1},{1,0},{2,3},{3,2},{4,5},{5,4},{6,7},{7,6},{8,9},{9,8},{10,11... | collective-permute-start | bytes 3145736 | tf_op jit(solution)/shard_map/ppermute | solution.py:480
  69.2 1.0 copy-start.3
  70.2 52.2 %all-to-all-start.2 = ((bf16[16,32,2048]{2,1,0:T(8,128)(2,1)}), bf16[16,32,2048]{2,1,0:T(8,128)(2,1)}, u32[]{:S(2)}, u32[]{:S(2)}) async-start(bf16[16,32,2048]{2,1,0:T(8,128)(2,1)} %get-tuple-element.55), calls=%async_computation.2 | async-start | bytes 4194304 | tf_op jit(solution)/shard_map/all_to_all | solution.py:435
  76.0 25.7 %collective-permute-start.1 = (bf16[16,16,2048]{2,1,0:T(8,128)(2,1)}, bf16[16,16,2048]{2,1,0:T(8,128)(2,1)S(1)}, u32[]{:S(2)}, u32[]{:S(2)}) collective-permute-start(bf16[16,16,2048]{2,1,0:T(8,128)(2,1)} %all-to-all-done.1.refs_2_), channel_id=1, source_target_pairs={{0,1},{1,0},{2,3},{3,2},{4,5},{5,4},{6,7},{7,6},{8,9},{9,8},{10,11... | collective-permute-start | bytes 3145736 | tf_op jit(solution)/shard_map/ppermute | solution.py:480
  101.7 1.0 copy-start.13
  102.6 1.2 copy-start.4
  122.3 57.7 %collective-permute-start.2 = (bf16[16,32,2048]{2,1,0:T(8,128)(2,1)}, bf16[16,32,2048]{2,1,0:T(8,128)(2,1)}, u32[]{:S(2)}, u32[]{:S(2)}) collective-permute-start(bf16[16,32,2048]{2,1,0:T(8,128)(2,1)} %all-to-all-done.2.refs_0_), channel_id=1, source_target_pairs={{0,1},{1,0},{2,3},{3,2},{4,5},{5,4},{6,7},{7,6},{8,9},{9,8},{10,11... | collective-permute-start | bytes 6291464 | tf_op jit(solution)/shard_map/ppermute | solution.py:480
  123.9 1.6 copy-start.8
  149.0 41.1 %all-to-all-start.3 = ((bf16[16,32,1152]{2,1,0:T(8,128)(2,1)}), bf16[16,32,1152]{2,1,0:T(8,128)(2,1)S(1)}, u32[]{:S(2)}, u32[]{:S(2)}) async-start(bf16[16,32,1152]{2,1,0:T(8,128)(2,1)} %bitcast.7), calls=%async_computation.3 | async-start | bytes 2359296 | tf_op jit(solution)/shard_map/all_to_all | solution.py:435
  154.9 1.6 copy-start.9
  188.7 1.3 copy-start.6
  190.1 40.4 %all-to-all-start.4 = ((bf16[16,32,1152]{2,1,0:T(8,128)(2,1)}), bf16[16,32,1152]{2,1,0:T(8,128)(2,1)S(1)}, u32[]{:S(2)}, u32[]{:S(2)}) async-start(bf16[16,32,1152]{2,1,0:T(8,128)(2,1)} %bitcast.8), calls=%async_computation.4 | async-start | bytes 2359296 | tf_op jit(solution)/shard_map/all_to_all | solution.py:435
  196.1 1.6 copy-start.7
  230.4 38.1 %copy-start.2 = (s32[16]{0:T(128)S(1)}, s32[16]{0:T(128)}, u32[]{:S(2)}) copy-start(s32[16]{0:T(128)} %order_ref.1) | copy-start | bytes 196
  264.1 29.5 %all-to-all-start.6 = ((bf16[16,32,1152]{2,1,0:T(8,128)(2,1)}), bf16[16,32,1152]{2,1,0:T(8,128)(2,1)}, u32[]{:S(2)}, u32[]{:S(2)}) async-start(bf16[16,32,1152]{2,1,0:T(8,128)(2,1)} %bitcast.10), calls=%async_computation.6 | async-start | bytes 2359296 | tf_op jit(solution)/shard_map/all_to_all | solution.py:435
  278.6 1.0 copy-start.5
  293.6 26.2 %collective-permute-start.3 = (bf16[512,1024]{1,0:T(8,128)(2,1)}, bf16[512,1024]{1,0:T(8,128)(2,1)S(1)}, u32[]{:S(2)}, u32[]{:S(2)}) collective-permute-start(bf16[512,1024]{1,0:T(8,128)(2,1)} %copy-done.5), channel_id=1, source_target_pairs={{0,1},{1,0},{2,3},{3,2},{4,5},{5,4},{6,7},{7,6},{8,9},{9,8},{10,11... | collective-permute-start | bytes 3145736 | tf_op jit(solution)/shard_map/ppermute | solution.py:552
  304.1 38.1 %collective-permute-start.4 = (bf16[512,1024]{1,0:T(8,128)(2,1)S(1)}, bf16[512,1024]{1,0:T(8,128)(2,1)S(1)}, u32[]{:S(2)}, u32[]{:S(2)}) collective-permute-start(bf16[512,1024]{1,0:T(8,128)(2,1)S(1)} %get-tuple-element.90), channel_id=1, source_target_pairs={{0,1},{1,0},{2,3},{3,2},{4,5},{5,4},{6,7},{7,6},{8,9},{9,8},{10,11... | collective-permute-start | bytes 3145736 | tf_op jit(solution)/shard_map/ppermute | solution.py:552
